TPU v7x, 128 devices: a whole 4x4x4 slice. The times are simulated.
128 devices in a mesh: replica: 16 (over x, z_lo, core), tensor: 8 (over z_hi, y).
Axes of the slice: x: 4, y: 4, z: 4 (z_hi: 2, z_lo: 2; z = z_hi * 2 + z_lo), core: 2. Of those that a mesh axis runs over, the one named last changes fastest.
Arguments:
- prompt: bfloat16 [16384, 6144], P('replica', 'tensor'), may hold values from -6 to 6
- dec_tokens: bfloat16 [64, 6144], P('replica', 'tensor'), may hold values from -6 to 6
- w_query: bfloat16 [6144, 6144], P(None, 'tensor'), may hold values from -0.078125 to 0.078125
- w_keyval: bfloat16 [6144, 2048], P(None, 'tensor'), may hold values from -0.078125 to 0.078125
- prefix_cache: bfloat16 [32, 1024, 2048], P('replica', None, 'tensor'), may hold values from -6 to 6
- prompt_len: int32 [32], replicated, may hold values from 256 to 512, as said below
- fill_len: int32 [32], replicated, may hold values from 256 to 1024, as said below
- owner: int32 [32], replicated, may hold values from 0 to 31, each once
Outputs:
- prefill_out: bfloat16 [16384, 6144], P('replica', 'tensor')
- decode_out: bfloat16 [64, 6144], P('replica', 'tensor')
- decode_cache: bfloat16 [32, 1536, 2048], P('replica', None, 'tensor')
Inputs may be any that keep to these rules, and one draw needn't show every extreme that they name: Each request's new prompt fills the first prompt_len slots of its 512; some request has 512 and some 512 // 2. `fill_len`: some request has 1024 and some 1024 // 4. `owner`: a permutation; decode row s lies on replica s // 2.
All inputs are finite; a program needn't handle non-finite values.
Results may differ from a plain program's by a relative error of at most 0.0095.
Values may be sent and summed in bfloat16 or wider, within the bound.
No kernel may reach another device: no remote copies, remote signals or barrier semaphores. Data moves between devices by JAX's collectives and lax.ppermute only.
A program may use at most 128 MiB of HBM per device.

v0:
```python
import math

import jax
import jax.numpy as jnp
from jax import lax
from jax.sharding import PartitionSpec as P

HEADS = 48
KV = 8
HD = 128


LOW_SCORE = -1e30
FULL_PREC = lax.Precision.HIGHEST


def prompt_head(query_rows, key_rows, values, fill_count, live_len):
    ctx_len = key_rows.shape[0] - query_rows.shape[0]
    score_scale = 1.0 / math.sqrt(query_rows.shape[1])
    scores = jnp.dot(query_rows, key_rows.T, preferred_element_type=jnp.float32) * score_scale
    key_pos = jnp.arange(key_rows.shape[0], dtype=jnp.int32)[None, :]
    query_pos = ctx_len + jnp.arange(query_rows.shape[0], dtype=jnp.int32)[:, None]
    inside = (key_pos < fill_count) | (key_pos >= ctx_len) & (key_pos <= query_pos) & (
        key_pos < ctx_len + live_len
    )
    masked = jnp.where(inside, scores, LOW_SCORE)
    row_top = jnp.max(masked, axis=1, keepdims=True)
    weights = jnp.where(inside, jnp.exp(masked - row_top), 0.0)
    row_total = jnp.sum(weights, axis=1, keepdims=True)
    attended = (
        jnp.dot(weights.astype(jnp.bfloat16), values, preferred_element_type=jnp.float32)
        / row_total
    )
    return jnp.where(query_pos < ctx_len + live_len, attended, 0.0).astype(jnp.bfloat16)


def prefill_heads(query_stack, cache_stack, fills, lengths):

    def per_pair(member):
        query_group, keyval, fill_count, live_len = member
        return lax.map(
            lambda query_rows: prompt_head(query_rows, keyval[0], keyval[1], fill_count, live_len),
            query_group,
        )

    return lax.map(per_pair, (query_stack, cache_stack, fills, lengths))


def combine(earlier, second):
    row_top = jnp.maximum(earlier[0], second[0])
    factor_one = jnp.exp(earlier[0] - row_top)
    factor_two = jnp.exp(second[0] - row_top)
    return (
        row_top,
        earlier[1] * factor_one + second[1] * factor_two,
        earlier[2] * factor_one[..., None] + second[2] * factor_two[..., None],
    )


def attend_part(query_rows, keyval, key_mask, score_scale):
    scores = (
        jnp.einsum("ntkgd,nskd->ntkgs", query_rows, keyval[:, :, :, 0], precision=FULL_PREC)
        * score_scale
    )
    wide_mask = key_mask[:, None, None, None, :]
    masked = jnp.where(wide_mask, scores, LOW_SCORE)
    row_top = jnp.max(masked, axis=4)
    weights = jnp.where(wide_mask, jnp.exp(masked - row_top[..., None]), 0.0)
    return (
        row_top,
        jnp.sum(weights, axis=4),
        jnp.einsum("ntkgs,nskd->ntkgd", weights, keyval[:, :, :, 1], precision=FULL_PREC),
    )


def live_mask(positions, fills, lives, ctx_len):
    return (positions[None, :] < fills[:, None]) | (positions[None, :] >= ctx_len) & (
        positions[None, :] < ctx_len + lives[:, None]
    )


def local(prompt, dec_tokens, w_query, w_keyval, prefix_cache, prompt_len, fill_len, owner):
    replicas = lax.axis_size("replica")
    replica_id = lax.axis_index("replica")
    per_rep = prefix_cache.shape[0]
    ctx_len = prefix_cache.shape[1]
    pair_cols = prefix_cache.shape[2]
    kv_here = pair_cols // (2 * HD)
    group_size = HEADS // KV
    new_len = prompt.shape[0] // per_rep
    dec_steps = dec_tokens.shape[0] // per_rep
    request_count = per_rep * replicas
    total_len = ctx_len + new_len
    block_len = total_len // replicas
    score_scale = 1.0 / math.sqrt(HD)
    first_req = replica_id * per_rep
    tok_piece = lax.all_gather(prompt, "tensor", axis=1, tiled=True)
    dec_piece = lax.all_gather(dec_tokens, "tensor", axis=1, tiled=True)
    queries = jnp.dot(tok_piece, w_query, preferred_element_type=jnp.float32).astype(jnp.bfloat16)
    keyvals = jnp.dot(tok_piece, w_keyval, preferred_element_type=jnp.float32).astype(jnp.bfloat16)
    dec_query = jnp.dot(dec_piece, w_query, preferred_element_type=jnp.float32).astype(jnp.bfloat16)
    dec_keyval = jnp.dot(dec_piece, w_keyval, preferred_element_type=jnp.float32).astype(
        jnp.bfloat16
    )
    full = jnp.concatenate([prefix_cache, keyvals.reshape(per_rep, new_len, pair_cols)], axis=1)
    local_fill = lax.dynamic_slice_in_dim(fill_len, first_req, per_rep, 0)
    local_live = lax.dynamic_slice_in_dim(prompt_len, first_req, per_rep, 0)
    positions = jnp.arange(total_len, dtype=jnp.int32)
    shipped = jnp.where(
        live_mask(positions, local_fill, local_live, ctx_len)[:, :, None],
        full,
        jnp.zeros((), full.dtype),
    )
    spread = lax.all_to_all(
        shipped.reshape(per_rep, replicas, block_len, pair_cols),
        "replica",
        split_axis=1,
        concat_axis=0,
        tiled=True,
    )
    spread = spread.reshape(request_count, block_len, pair_cols)
    query_stack = (
        queries.reshape(per_rep, new_len, kv_here, group_size, HD)
        .transpose(0, 2, 3, 1, 4)
        .reshape(per_rep * kv_here, group_size, new_len, HD)
    )
    cache_stack = (
        full.reshape(per_rep, total_len, kv_here, 2, HD)
        .transpose(0, 2, 3, 1, 4)
        .reshape(per_rep * kv_here, 2, total_len, HD)
    )
    attended = prefill_heads(
        query_stack, cache_stack, jnp.repeat(local_fill, kv_here), jnp.repeat(local_live, kv_here)
    )
    prefill_out = (
        attended.reshape(per_rep, kv_here, group_size, new_len, HD)
        .transpose(0, 3, 1, 2, 4)
        .reshape(per_rep * new_len, kv_here * group_size * HD)
    )
    slot_ids = jnp.arange(request_count, dtype=jnp.int32)
    source = jnp.sum(jnp.where(owner[None, :] == slot_ids[:, None], slot_ids[None, :], 0), axis=1)
    by_slot = jnp.take(spread, source, axis=0)
    homed = lax.all_to_all(
        by_slot.reshape(replicas, per_rep, block_len, pair_cols),
        "replica",
        split_axis=0,
        concat_axis=2,
        tiled=True,
    )
    decode_cache = homed.reshape(per_rep, total_len, pair_cols)
    own_query = dec_query.reshape(per_rep, dec_steps, kv_here, group_size, HD).astype(jnp.float32)
    own_kv = dec_keyval.reshape(per_rep, dec_steps, kv_here, 2, HD).astype(jnp.float32)
    causal = (jnp.arange(dec_steps)[None, :] <= jnp.arange(dec_steps)[:, None])[
        None, :, None, None, :
    ]
    fresh_scores = (
        jnp.einsum("ctkgd,cukd->ctkgu", own_query, own_kv[..., 0, :], precision=FULL_PREC)
        * score_scale
    )
    fresh_scores = jnp.where(causal, fresh_scores, LOW_SCORE)
    fresh_top = jnp.max(fresh_scores, axis=4)
    fresh_w = jnp.where(causal, jnp.exp(fresh_scores - fresh_top[..., None]), 0.0)
    own_part = (
        fresh_top,
        jnp.sum(fresh_w, axis=4),
        jnp.einsum("ctkgu,cukd->ctkgd", fresh_w, own_kv[..., 1, :], precision=FULL_PREC),
    )
    my_source = lax.dynamic_slice_in_dim(source, first_req, per_rep, 0)
    slot_mask = live_mask(
        positions, jnp.take(fill_len, my_source), jnp.take(prompt_len, my_source), ctx_len
    )
    held_cache = decode_cache.reshape(per_rep, total_len, kv_here, 2, HD).astype(jnp.float32)
    joined = combine(attend_part(own_query, held_cache, slot_mask, score_scale), own_part)
    totals = joined[1]
    weighted_sum = joined[2]
    decode_out = (
        (weighted_sum / totals[..., None])
        .reshape(per_rep * dec_steps, kv_here * group_size * HD)
        .astype(jnp.bfloat16)
    )
    return (prefill_out, decode_out, decode_cache)


def solution(mesh):
    in_specs = (
        P("replica", "tensor"),
        P("replica", "tensor"),
        P(None, "tensor"),
        P(None, "tensor"),
        P("replica", None, "tensor"),
        P(),
        P(),
        P(),
    )
    out_specs = (P("replica", "tensor"), P("replica", "tensor"), P("replica", None, "tensor"))
    return jax.shard_map(local, mesh=mesh, in_specs=in_specs, out_specs=out_specs, check_vma=False)
```

profile of v0, /device:TPU:1, one launch (start us, length us, event | category | flops | bytes accessed | tf_op | source)
XLA Modules:
  0.0 318.8 jit_solution(11955704828881061122)
XLA Ops:
  12.4 30.3 %all_gather.7 = bf16[4,6144]{1,0:T(4,128)(2,1)S(1)} all-gather(bf16[4,768]{1,0:T(4,128)(2,1)S(1)} %copy-done.16), channel_id=1, replica_groups=mesh['replica'=16,'tensor'=8] {'tensor'}, dimensions={1}, use_global_device_ids=true | all-gather | bytes 55296 | tf_op jit(solution)/shard_map/all_gather | solution.py:98
  42.6 5.0 %convolution_convert_fusion.2 = bf16[4,768]{1,0:T(4,128)(2,1)S(1)} fusion(bf16[4,6144]{1,0:T(4,128)(2,1)S(1)} %all_gather.7, bf16[6144,768]{1,0:T(8,128)(2,1)} %param.16), kind=kOutput, calls=%fused_computation.54 | convolution fusion | flops 37751808 | bytes 9492480 | tf_op jit(solution)/shard_map/dot_general | solution.py:101
  52.9 106.5 %all-gather.2.cloned.1.call-done = bf16[1024,6144]{1,0:T(8,128)(2,1)} async-done(((bf16[1024,768]{1,0:T(8,128)(2,1)}), bf16[1024,6144]{1,0:T(8,128)(2,1)}) %all-gather.2.cloned.1.call-update) | async-done | bytes 12582928 | tf_op jit(solution)/shard_map/all_gather | solution.py:97
  159.4 6.5 %convolution_convert_fusion.1 = bf16[1024,256]{1,0:T(8,128)(2,1)S(1)} fusion(bf16[1024,6144]{1,0:T(8,128)(2,1)} %all-gather.2.cloned.1.call-done, bf16[6144,256]{1,0:T(8,128)(2,1)S(1)} %copy-done), kind=kOutput, calls=%fused_computation.46 | convolution fusion | flops 3221487616 | bytes 16252928 | tf_op jit(solution)/shard_map/dot_general | solution.py:100
  168.1 5.4 %all-to-all-start = ((bf16[2,16,96,256]{3,2,0,1:T(8,128)(2,1)}), bf16[2,16,96,256]{3,2,0,1:T(8,128)(2,1)}, u32[]{:S(2)}, u32[]{:S(2)}) async-start(bf16[2,16,96,256]{3,2,0,1:T(8,128)(2,1)} %copy.71), calls=%async_computation | async-start | bytes 3145728 | tf_op jit(solution)/shard_map/all_to_all | solution.py:114
  173.5 14.5 %convolution_convert_fusion = bf16[1024,768]{1,0:T(8,128)(2,1)S(1)} fusion(bf16[1024,6144]{1,0:T(8,128)(2,1)} %all-gather.2.cloned.1.call-done, bf16[6144,768]{1,0:T(8,128)(2,1)} %param.16), kind=kOutput, calls=%fused_computation.40 | convolution fusion | flops 9664462848 | bytes 23592960 | tf_op jit(solution)/shard_map/dot_general | solution.py:99
  190.9 2.9 copy.68
  198.9 5.7 %all-to-all-start.1 = ((bf16[16,2,96,256]{3,2,1,0:T(8,128)(2,1)}), bf16[16,2,96,256]{3,2,1,0:T(8,128)(2,1)}, u32[]{:S(2)}, u32[]{:S(2)}) async-start(bf16[16,2,96,256]{3,2,1,0:T(8,128)(2,1)} %broadcast_select_fusion.1), calls=%async_computation.1 | async-start | bytes 3145728 | tf_op jit(solution)/shard_map/all_to_all | solution.py:143
  204.7 92.3 %while.23 = (s32[]{:T(128)}, bf16[2,6,512,128]{3,2,1,0:T(8,128)(2,1)}, bf16[2,6,512,128]{3,2,1,0:T(8,128)(2,1)}, bf16[2,2,1536,128]{2,3,1,0:T(8,128)(2,1)}, s32[...) while((s32[]{:T(128)}, bf16[2,6,512,128]{3,2,1,0:T(8,128)(2,1)}, ...), condition=%wide.region_5.6_spmd, body=%wide.region_0.5_spmd.sunk | while | flops 419369984 | bytes 19962720 | solution.py:46
  211.0 37.8 %while.24 = (s32[]{:T(128)}, bf16[6,512,128]{2,1,0:T(8,128)(2,1)}, s32[]{:T(128)}, s32[]{:T(128)}, bf16[6,512,128]{2,1,0:T(8,128)(2,1)}, /*index=5*/bf16[2,1536,128]{2,1,0:T(8,128)(2,1)}, s32[]{:T(128)}) while((s32[]{:T(128)}, bf16[6,512,128]{2,1,0:T(8,128)(2,1)}, s32[]{:T(128)}, s32[]{:T(128)}, bf16[6,512,128]{2,1,0:T(8,128)(2,1)}, ...), condition=%wide.region_4.4_spmd, body=%wide.region_1.3_spmd.sunk | while | flops 419369984 | bytes 13671045 | solution.py:41
  211.6 2.3 fusion.77
  217.9 2.3 fusion.77
  224.2 2.3 fusion.77
  230.5 2.3 fusion.77
  236.8 2.3 fusion.77
  243.1 2.3 fusion.77
  257.2 37.8 %while.24 = (s32[]{:T(128)}, bf16[6,512,128]{2,1,0:T(8,128)(2,1)}, s32[]{:T(128)}, s32[]{:T(128)}, bf16[6,512,128]{2,1,0:T(8,128)(2,1)}, /*index=5*/bf16[2,1536,128]{2,1,0:T(8,128)(2,1)}, s32[]{:T(128)}) while((s32[]{:T(128)}, bf16[6,512,128]{2,1,0:T(8,128)(2,1)}, s32[]{:T(128)}, s32[]{:T(128)}, bf16[6,512,128]{2,1,0:T(8,128)(2,1)}, ...), condition=%wide.region_4.4_spmd, body=%wide.region_1.3_spmd.sunk | while | flops 419369984 | bytes 13671045 | solution.py:41
  257.8 2.4 fusion.77
  264.1 2.4 fusion.77
  270.4 2.3 fusion.77
  276.7 2.3 fusion.77
  289.3 2.3 fusion.77
  297.0 2.5 copy.85
  305.5 4.4 %fusion.58 = (bf16[2,1536,1,1,128]{4,3,1,0,2:T(2,128)(2,1)S(1)}, bf16[2,1536,1,1,128]{4,3,1,0,2:T(2,128)(2,1)S(1)}) fusion(bf16[2,1536,1,2,128]{4,3,1,0,2:T(2,128)(2,1)} %reshape_reshape.3), kind=kLoop, calls=%fused_computation.100 | loop fusion | bytes 3145728 | tf_op jit(solution)/shard_map/slice | solution.py:62
  (196 shorter events, 93.1 us)
Async XLA Ops:
  7.2 42.9 %copy-start = (bf16[6144,256]{1,0:T(8,128)(2,1)S(1)}, bf16[6144,256]{1,0:T(8,128)(2,1)}, u32[]{:S(2)}) copy-start(bf16[6144,256]{1,0:T(8,128)(2,1)} %param.17) | copy-start | bytes 9437188
  7.2 4.4 %copy-start.2 = (s32[32]{0:T(128)S(1)}, s32[32]{0:T(128)}, u32[]{:S(2)}) copy-start(s32[32]{0:T(128)} %param.20) | copy-start | bytes 388
  7.2 5.2 %copy-start.16 = (bf16[4,768]{1,0:T(4,128)(2,1)S(1)}, bf16[4,768]{1,0:T(4,128)(2,1)}, u32[]{:S(2)}) copy-start(bf16[4,768]{1,0:T(4,128)(2,1)} %param.15) | copy-start | bytes 18436
  7.2 152.2 %all-gather.2.cloned.1.call-start = ((), (), s32[]{:S(2)}) async-start(), calls=%async_computation.2 | async-start | bytes 14155776 | tf_op jit(solution)/shard_map/all_gather | solution.py:97
  47.7 2.9 copy-start.10
  50.6 115.4 %copy-start.17 = (bf16[4,256]{1,0:T(4,128)(2,1)}, bf16[4,256]{1,0:T(4,128)(2,1)S(1)}, u32[]{:S(2)}) copy-start(bf16[4,256]{1,0:T(4,128)(2,1)S(1)} %convolution_convert_fusion.3) | copy-start | bytes 6148
  159.4 6.6 %copy-start.5 = (bf16[2,1024,256]{2,1,0:T(8,128)(2,1)S(1)}, bf16[2,1024,256]{2,1,0:T(8,128)(2,1)}, u32[]{:S(2)}) copy-start(bf16[2,1024,256]{2,1,0:T(8,128)(2,1)} %param.18) | copy-start | bytes 3145732
  168.1 27.4 %all-to-all-start = ((bf16[2,16,96,256]{3,2,0,1:T(8,128)(2,1)}), bf16[2,16,96,256]{3,2,0,1:T(8,128)(2,1)}, u32[]{:S(2)}, u32[]{:S(2)}) async-start(bf16[2,16,96,256]{3,2,0,1:T(8,128)(2,1)} %copy.71), calls=%async_computation | async-start | bytes 3145728 | tf_op jit(solution)/shard_map/all_to_all | solution.py:114
  173.5 14.5 %copy-start.9 = (bf16[1024,256]{1,0:T(8,128)(2,1)S(1)}, bf16[1024,256]{1,0:T(8,128)(2,1)}, u32[]{:S(2)}) copy-start(bf16[1024,256]{1,0:T(8,128)(2,1)} %copy-done.8) | copy-start | bytes 1572868
  190.9 2.9 copy-start.7
  190.9 3.3 %copy-start.6 = (bf16[2,1024,256]{1,2,0:T(8,128)(2,1)S(1)}, bf16[2,1024,256]{1,2,0:T(8,128)(2,1)}, u32[]{:S(2)}) copy-start(bf16[2,1024,256]{1,2,0:T(8,128)(2,1)} %copy.66) | copy-start | bytes 3145732
  198.9 102.0 %all-to-all-start.1 = ((bf16[16,2,96,256]{3,2,1,0:T(8,128)(2,1)}), bf16[16,2,96,256]{3,2,1,0:T(8,128)(2,1)}, u32[]{:S(2)}, u32[]{:S(2)}) async-start(bf16[16,2,96,256]{3,2,1,0:T(8,128)(2,1)} %broadcast_select_fusion.1), calls=%async_computation.1 | async-start | bytes 3145728 | tf_op jit(solution)/shard_map/all_to_all | solution.py:143
  214.0 1.4 copy-start.3
  220.3 1.4 copy-start.3
  226.6 1.4 copy-start.3
  232.9 1.4 copy-start.3
  239.1 1.4 copy-start.3
  245.4 1.4 copy-start.3
  260.1 1.4 copy-start.3
  305.5 4.5 %copy-start.11 = (bf16[2,2,6,128]{3,2,1,0:T(8,128)(2,1)S(1)}, bf16[2,2,6,128]{3,2,1,0:T(8,128)(2,1)}, u32[]{:S(2)}) copy-start(bf16[2,2,6,128]{3,2,1,0:T(8,128)(2,1)} %copy-done.10) | copy-start | bytes 18436
  305.5 4.5 %copy-start.12 = (pred[2,1536]{1,0:T(4,128)(4,1)S(1)}, pred[2,1536]{1,0:T(4,128)(4,1)}, u32[]{:S(2)}) copy-start(pred[2,1536]{1,0:T(4,128)(4,1)} %and_or_fusion) | copy-start | bytes 9220
  305.5 5.1 %copy-start.14 = (f32[2,2,6]{2,1,0:T(2,128)S(1)}, f32[2,2,6]{2,1,0:T(2,128)}, u32[]{:S(2)}) copy-start(f32[2,2,6]{2,1,0:T(2,128)} %copy-done.13) | copy-start | bytes 292
  305.5 5.1 %copy-start.15 = (f32[2,2,6]{2,1,0:T(2,128)S(1)}, f32[2,2,6]{2,1,0:T(2,128)}, u32[]{:S(2)}) copy-start(f32[2,2,6]{2,1,0:T(2,128)} %get-tuple-element.172) | copy-start | bytes 292
  305.5 6.4 %copy-start.1 = (bf16[6144,256]{1,0:T(8,128)(2,1)S(1)}, bf16[6144,256]{1,0:T(8,128)(2,1)}, u32[]{:S(2)}) copy-start(bf16[6144,256]{1,0:T(8,128)(2,1)} %param.17) | copy-start | bytes 9437188
  (10 other events, 12.8 us)
Sparse Core Ops, SparseCore 0:
  10.3 149.0 all-gather.1
where the time goes:
time: 320 us; the launch traced here: 319 us
  waiting for transfers between devices  107 us (33%)
  matrix products  79 us (25%)
  local copies, waits for them, and re-layouts  43.9 us (14%)
  other arithmetic  31.2 us (10%)
  blocking collectives  30.3 us (9%)
  between operations  14.4 us (4%)
  starting transfers between devices  11.2 us (4%)
    all_gather x1, waiting for transfers between devices, local(): tok_piece = lax.all_gather(prompt, 'tensor', axis=1, tiled=True)  107 us
    all_gather x1, blocking collectives, local(): dec_piece = lax.all_gather(dec_tokens, 'tensor', axis=1, tiled=True)  30.3 us
    dot_general x12, matrix products, prompt_head(): jnp.dot(query_rows, key_rows.T, preferred_element_type=jnp.float32)  28.2 us
    dot_general x12, matrix products, prompt_head(): jnp.dot(weights.astype(jnp.bfloat16), values, preferred_element_type=jnp....  23 us
    reduce_sum x12, other arithmetic, prompt_head(): row_total = jnp.sum(weights, axis=1, keepdims=True)  16.9 us
    dot_general x1, matrix products, local(): jnp.dot(tok_piece, w_query, preferred_element_type=jnp.float32)  14.5 us
    unnamed x42, local copies, waits for them, and re-layouts  8.15 us
    dynamic_slice x8, local copies, waits for them, and re-layouts, prefill_heads(): return lax.map(per_pair, (query_stack, cache_stack, fills, lengths))  7.21 us
  transfers between devices with their start and end apart: 3, of which 1 were waited for; matrix products, arithmetic and copies ran while one was open for 41% of the time, Pallas kernels for 0%

commit v1 on v0

v1 whole, which is shorter than its diff:
```python
import functools
import math

import jax
import jax.numpy as jnp
from jax import lax
from jax.experimental import pallas as pl
from jax.experimental.pallas import tpu as pltpu
from jax.sharding import PartitionSpec as P

HEADS = 48
KV = 8
HD = 128
GROUP = HEADS // KV
STEPS = 2
DEC_ROWS = 16
KEY_BLOCK = 256
MIB = 1024 * 1024

LOW_SCORE = -1e30
EXP_SCALE = math.log2(math.e) / math.sqrt(HD)


def dot_nt(a, b):
    return lax.dot_general(a, b, (((1,), (1,)), ((), ())), preferred_element_type=jnp.float32)


def dot_nn(a, b):
    return lax.dot_general(a, b, (((1,), (0,)), ((), ())), preferred_element_type=jnp.float32)


def row_tiles(counts):
    tiles = []
    start = 0
    for count in counts:
        first = (count // 2 + 15) // 16 * 16
        tiles += [(start, first), (start + first, count - first)]
        start += count
    return tiles


def project_kernel(shape, has_start, widths, ids, *refs):
    groups, counts, depth = shape
    refs = list(refs)
    pieces = [[refs.pop(0) for _ in counts] for _ in range(groups)]
    weights = [refs.pop(0) for _ in widths]
    start_ref = refs.pop(0) if has_start else None
    held, weight_held, total, sems = refs[-4:]
    outs = refs[:-4]
    offsets = [sum(counts[:i]) for i in range(len(counts))]
    columns = [sum(widths[:i]) for i in range(len(widths))]
    per = 1

    def copies(k):
        made = []
        for j in range(k * per, (k + 1) * per):
            at = pl.ds((j - k * per) * depth, depth)
            for i, count in enumerate(counts):
                made.append((pieces[j][i], held.at[k, pl.ds(offsets[i], count), at]))
            half = depth // 2
            for i, width in enumerate(widths):
                for part in range(2):
                    src = pl.ds(pl.multiple_of(ids[j] * depth + part * half, half), half)
                    dst = pl.ds((j - k * per) * depth + part * half, half)
                    made.append(
                        (
                            weights[i].at[src, :],
                            weight_held.at[k, dst, pl.ds(columns[i], width)],
                        )
                    )
        return [
            pltpu.make_async_copy(src, dst, sems.at[k, n]) for n, (src, dst) in enumerate(made)
        ]

    steps = groups // per
    for k in range(steps):
        for copy in copies(k):
            copy.start()
    all_columns = sum(widths)
    for k in range(steps):
        for copy in copies(k):
            copy.wait()
        for row, count in row_tiles(counts):
            for col in range(0, all_columns, 512):
                width = min(512, all_columns - col)
                at = (slice(row, row + count), slice(col, col + width))
                part = dot_nn(held[k, row : row + count, :], weight_held[k, :, col : col + width])
                if k:
                    part = part + total[at]
                elif has_start:
                    part = part + start_ref[row : row + count, col : col + width]
                if k < steps - 1:
                    total[at] = part
                    continue
                if outs[0].dtype == jnp.float32:
                    group = max(i for i, offset in enumerate(offsets) if offset <= row)
                    low = row - offsets[group]
                    outs[group][low : low + count, col : col + width] = part
                    continue
                for out, first, wide in zip(outs, columns, widths):
                    low, high = max(first, col), min(first + wide, col + width)
                    if low < high:
                        value = part[:, low - col : high - col].astype(jnp.bfloat16)
                        out[row : row + count, low - first : high - first] = value


def project(pieces, ids, weights, start=None, start_col=0, out_type=jnp.bfloat16):
    groups = len(pieces)
    counts = tuple(x.shape[0] for x in pieces[0])
    depth = pieces[0][0].shape[1]
    widths = tuple(w.shape[1] for w in weights)
    rows, columns = sum(counts), sum(widths)
    has_start = start is not None
    operands = [x for group in pieces for x in group] + list(weights)
    in_specs = [pl.BlockSpec(memory_space=pltpu.HBM)] * len(operands)
    if has_start:
        in_specs.append(pl.BlockSpec((rows, columns), lambda *_: (0, start_col // columns)))
        operands.append(start)
    if out_type == jnp.float32:
        out_shape = [jax.ShapeDtypeStruct((count, columns), jnp.float32) for count in counts]
    else:
        out_shape = [jax.ShapeDtypeStruct((rows, w), jnp.bfloat16) for w in widths]
    per = 1
    copies = per * (len(counts) + 2 * len(widths))
    return pl.pallas_call(
        functools.partial(
            project_kernel, (groups, counts, depth), has_start, widths
        ),
        out_shape=out_shape,
        grid_spec=pltpu.PrefetchScalarGridSpec(
            num_scalar_prefetch=1,
            grid=(1,),
            in_specs=in_specs,
            out_specs=[pl.BlockSpec(memory_space=pltpu.VMEM)] * len(out_shape),
            scratch_shapes=[
                pltpu.VMEM((groups // per, rows, per * depth), jnp.bfloat16),
                pltpu.VMEM((groups // per, per * depth, columns), jnp.bfloat16),
                pltpu.VMEM((rows, columns), jnp.float32),
                pltpu.SemaphoreType.DMA((groups // per, copies)),
            ],
        ),
        compiler_params=pltpu.CompilerParams(
            dimension_semantics=("arbitrary",), vmem_limit_bytes=40 * MIB
        ),
        cost_estimate=pl.CostEstimate(
            flops=2 * rows * depth * groups * columns,
            bytes_accessed=2 * groups * depth * (rows + columns) + 4 * rows * columns,
            transcendentals=0,
        ),
        name="project",
    )(ids, *operands)


def pack_kernel(reqs, first_pos, live_ref, kv_ref, *refs):
    out_ref = refs[-1]
    dests, length, columns = out_ref.shape
    each = kv_ref.shape[0] // reqs // 16 * 16
    block = each // dests
    pos = first_pos + lax.broadcasted_iota(jnp.int32, (each, 1), 0)
    for req in range(reqs):
        rows = kv_ref[req * each : (req + 1) * each, :]
        rows = jnp.where(pos < live_ref[req], rows, jnp.zeros_like(rows))
        for dest in range(dests):
            out_ref[dest, req * block : (req + 1) * block, :] = rows[
                dest * block : (dest + 1) * block
            ]
    if len(refs) == 1:
        return
    q_ref = refs[0]
    count = length - reqs * block
    per = q_ref.shape[1] // columns + 1
    at = reqs * each
    queries = q_ref[...].astype(jnp.float32)
    keyvals = kv_ref[at : at + q_ref.shape[0], :].astype(jnp.float32)
    slab = []
    for row in range(count // per):
        for part in range(per - 1):
            slab.append(queries[row : row + 1, part * columns : (part + 1) * columns])
        slab.append(keyvals[row : row + 1, :])
    slab = jnp.concatenate(slab, axis=0).astype(jnp.bfloat16)
    for dest in range(dests):
        out_ref[dest, reqs * block :, :] = slab


def pack(keyvals, reqs, first_pos, lives, dests, queries=None):
    columns = keyvals.shape[1]
    each = keyvals.shape[0] // reqs // 16 * 16
    length = reqs * each // dests
    operands = [keyvals]
    in_specs = [pl.BlockSpec(memory_space=pltpu.VMEM)]
    if queries is not None:
        length += reqs * STEPS * (queries.shape[1] // columns + 1)
        operands.append(queries)
        row = reqs * each // DEC_ROWS
        in_specs.append(pl.BlockSpec((DEC_ROWS, queries.shape[1]), lambda *_: (row, 0)))
    return pl.pallas_call(
        functools.partial(pack_kernel, reqs, first_pos),
        out_shape=jax.ShapeDtypeStruct((dests, length, columns), keyvals.dtype),
        grid_spec=pltpu.PrefetchScalarGridSpec(
            num_scalar_prefetch=1,
            grid=(1,),
            in_specs=in_specs,
            out_specs=pl.BlockSpec(memory_space=pltpu.VMEM),
        ),
        compiler_params=pltpu.CompilerParams(vmem_limit_bytes=16 * MIB),
        cost_estimate=pl.CostEstimate(
            flops=0, bytes_accessed=4 * dests * length * columns, transcendentals=0
        ),
        name="pack",
    )(lives, *operands)


def route_kernel(block, count, source, *refs):
    got_refs, out_ref = refs[:count], refs[-1]
    dests = out_ref.shape[0]
    per_rep = source.shape[0] // dests
    for slot in range(source.shape[0]):
        request = source[slot]
        at = pl.ds(pl.multiple_of((request % per_rep) * block, block), block)
        for part in range(count):
            low = (part * per_rep + slot % per_rep) * block
            out_ref[slot // per_rep, low : low + block, :] = got_refs[part][
                request // per_rep, at, :
            ]
    low = count * per_rep * block
    for extra_ref in refs[count:-1]:
        for dest in range(dests):
            out_ref[dest, low : low + extra_ref.shape[0], :] = extra_ref[...]


def route(got, source, block, *extra):
    dests, _, columns = got[0].shape
    per_rep = source.shape[0] // dests
    length = len(got) * per_rep * block + sum(x.shape[0] for x in extra)
    operands = [*got, *extra]
    return pl.pallas_call(
        functools.partial(route_kernel, block, len(got)),
        out_shape=jax.ShapeDtypeStruct((dests, length, columns), got[0].dtype),
        grid_spec=pltpu.PrefetchScalarGridSpec(
            num_scalar_prefetch=1,
            grid=(1,),
            in_specs=[pl.BlockSpec(memory_space=pltpu.VMEM)] * len(operands),
            out_specs=pl.BlockSpec(memory_space=pltpu.VMEM),
        ),
        compiler_params=pltpu.CompilerParams(vmem_limit_bytes=16 * MIB),
        cost_estimate=pl.CostEstimate(
            flops=0, bytes_accessed=4 * dests * length * columns, transcendentals=0
        ),
        name="route",
    )(source, *operands)


def finish_kernel(block, count, source, home_ref, earlier_ref, cache_ref, out_ref):
    dests, _, columns = home_ref.shape
    per_rep = out_ref.shape[0] // STEPS
    slot = pl.program_id(0)
    for part in range(count):
        at = pl.ds(pl.multiple_of((part * per_rep + slot) * block, block), block)
        for dest in range(dests):
            low = (part * dests + dest) * block
            cache_ref[0, low : low + block, :] = home_ref[dest, at, :]

    @pl.when(slot == 0)
    def _():
        low = count * per_rep * block
        for mine in range(per_rep):
            request = source[mine]
            both = home_ref[request // per_rep, low : low + 16, :].astype(jnp.float32)
            rows = jnp.where(request % per_rep == 0, both[:8], both[8:])
            for step in range(STEPS):
                for part in range(out_ref.shape[1] // columns):
                    row = step * (8 // STEPS) + part
                    at = mine * STEPS + step
                    out_ref[at : at + 1, part * columns : (part + 1) * columns] = rows[
                        row : row + 1
                    ].astype(jnp.bfloat16)


def finish(home, earlier, source, block, count, q_cols):
    dests, _, columns = home.shape
    per_rep, total_len, _ = earlier.shape
    new_len = count * dests * block
    return pl.pallas_call(
        functools.partial(finish_kernel, block, count),
        out_shape=(
            jax.ShapeDtypeStruct(earlier.shape, earlier.dtype),
            jax.ShapeDtypeStruct((per_rep * STEPS, q_cols), earlier.dtype),
        ),
        grid_spec=pltpu.PrefetchScalarGridSpec(
            num_scalar_prefetch=1,
            grid=(per_rep,),
            in_specs=[
                pl.BlockSpec(memory_space=pltpu.VMEM),
                pl.BlockSpec(memory_space=pltpu.HBM),
            ],
            out_specs=(
                pl.BlockSpec((1, new_len, columns), lambda c, *_: (c, total_len // new_len - 1, 0)),
                pl.BlockSpec(memory_space=pltpu.VMEM),
            ),
        ),
        input_output_aliases={2: 0},
        compiler_params=pltpu.CompilerParams(vmem_limit_bytes=16 * MIB),
        name="finish",
    )(source, home, earlier)


def phase_end(*arrays):
    return lax.optimization_barrier(arrays)


def prefill_kernel(parts, ctx_len, fill_ref, live_ref, q_ref, prefix_ref, *refs):
    kv_refs = refs[: parts + 1]
    out_ref = refs[-1]
    req = pl.program_id(0)
    fill = fill_ref[req]
    live = live_ref[req]
    rows = q_ref.shape[0]
    first_row = parts * rows
    row_ids = lax.broadcasted_iota(jnp.int32, (rows, 1), 0)
    own_ids = lax.broadcasted_iota(jnp.int32, (rows, rows), 1)
    causal = own_ids <= lax.broadcasted_iota(jnp.int32, (rows, rows), 0)

    def heads(blocks):
        seen = blocks * KEY_BLOCK
        last = seen - KEY_BLOCK
        last_live = last + lax.broadcasted_iota(jnp.int32, (rows, KEY_BLOCK), 1) < fill

        def one_head(h):
            cols = pl.ds(pl.multiple_of(h * HD, HD), HD)
            query = q_ref[:, cols]
            scores = []
            if last:
                scores.append(dot_nt(query, prefix_ref[0, :last, :HD]))
            scores.append(
                jnp.where(last_live, dot_nt(query, prefix_ref[0, last:seen, :HD]), LOW_SCORE)
            )
            for part in range(parts):
                scores.append(dot_nt(query, kv_refs[part][:, :HD]))
            scores.append(jnp.where(causal, dot_nt(query, kv_refs[parts][:, :HD]), LOW_SCORE))
            top = scores[0].max(axis=1, keepdims=True)
            for score in scores[1:]:
                top = jnp.maximum(top, score.max(axis=1, keepdims=True))
            weights = [jnp.exp2((score - top) * EXP_SCALE) for score in scores]
            total = weights[0].sum(axis=1, keepdims=True)
            for weight in weights[1:]:
                total = total + weight.sum(axis=1, keepdims=True)
            weights = [weight.astype(jnp.bfloat16) for weight in weights]
            mixed = None
            values = []
            if last:
                values.append(prefix_ref[0, :last, HD:])
            values.append(prefix_ref[0, last:seen, HD:])
            for part in range(parts + 1):
                values.append(kv_refs[part][:, HD:])
            for weight, value in zip(weights, values):
                term = dot_nn(weight, value)
                mixed = term if mixed is None else mixed + term
            mixed = mixed / total
            if parts:
                mixed = jnp.where(first_row + row_ids < live, mixed, 0.0)
            out_ref[:, cols] = mixed.astype(jnp.bfloat16)

        @pl.loop(0, GROUP // 2)
        def _(pair):
            one_head(2 * pair)
            one_head(2 * pair + 1)

    block_count = (fill + KEY_BLOCK - 1) // KEY_BLOCK
    is_live = first_row < live
    for blocks in range(1, ctx_len // KEY_BLOCK + 1):

        @pl.when((block_count == blocks) & is_live)
        def _(blocks=blocks):
            heads(blocks)

    @pl.when(jnp.logical_not(is_live))
    def _():
        out_ref[...] = jnp.zeros_like(out_ref)


def prefill_part(part, part_count, queries, prefix, keyvals, fills, lives, earlier_out):
    cols = queries.shape[1]
    reqs, ctx_len, pair_cols = prefix.shape
    rows = queries.shape[0] // reqs // 16 * 16
    in_specs = [
        pl.BlockSpec((rows, cols), lambda r, *_: (r, 0)),
        pl.BlockSpec((1, ctx_len, pair_cols), lambda r, *_: (r, 0, 0)),
    ]
    in_specs += [pl.BlockSpec((rows, pair_cols), lambda r, *_: (r, 0))] * (part + 1)
    operands = [queries, prefix, *keyvals[: part + 1]]
    aliases = {}
    if earlier_out is not None:
        in_specs.append(pl.BlockSpec(memory_space=pl.ANY))
        aliases = {2 + len(operands): 0}
        operands.append(earlier_out)
    return pl.pallas_call(
        functools.partial(prefill_kernel, part, ctx_len),
        out_shape=jax.ShapeDtypeStruct((reqs * part_count * rows, cols), jnp.bfloat16),
        grid_spec=pltpu.PrefetchScalarGridSpec(
            num_scalar_prefetch=2,
            grid=(reqs,),
            in_specs=in_specs,
            out_specs=pl.BlockSpec((rows, cols), lambda r, *_: (r * part_count + part, 0)),
        ),
        input_output_aliases=aliases,
        compiler_params=pltpu.CompilerParams(
            dimension_semantics=("arbitrary",), vmem_limit_bytes=24 * MIB
        ),
        cost_estimate=pl.CostEstimate(
            flops=4 * reqs * rows * cols * (ctx_len + rows),
            bytes_accessed=2 * reqs * (2 * rows * cols + ctx_len * pair_cols),
            transcendentals=reqs * rows * (cols // HD) * (ctx_len + rows),
        ),
        name="prefill",
    )(fills, lives, *operands)


def decode_kernel(parts, held, owner_ref, fill_ref, live_ref, got_ref, prefix_ref, *refs):
    kv_refs = refs[:parts]
    out_ref = refs[-1]
    reqs = prefix_ref.shape[0]
    ctx_len = prefix_ref.shape[1]
    part_len = kv_refs[0].shape[0] // reqs // 16 * 16
    half = out_ref.shape[0] // reqs

    def live_where(count, limit, scores):
        return jnp.where(
            lax.broadcasted_iota(jnp.int32, scores.shape, 1) < limit, scores, LOW_SCORE
        )

    for req in range(reqs):
        slot = owner_ref[req]
        fill = fill_ref[req]
        live = live_ref[req]
        both = got_ref[slot // reqs, held : held + 2 * half, :].astype(jnp.float32)
        slab = jnp.where(slot % reqs == 0, both[:half], both[half:])
        query = jnp.concatenate([slab[:, :HD], slab[:, HD:]], axis=0).astype(jnp.bfloat16)
        rows = query.shape[0]
        scores = [live_where(ctx_len, fill, dot_nt(query, prefix_ref[req, :, :HD]))]
        values = [prefix_ref[req, :, HD:]]
        for part in range(parts):
            part_scores = dot_nt(query, kv_refs[part][req * part_len : (req + 1) * part_len, :HD])
            scores.append(live_where(part_len, live - part * part_len, part_scores))
            values.append(kv_refs[part][req * part_len : (req + 1) * part_len, HD:])
        own_scores = dot_nt(query, query)
        row_ids = lax.broadcasted_iota(jnp.int32, own_scores.shape, 0)
        key_ids = lax.broadcasted_iota(jnp.int32, own_scores.shape, 1)
        per_step = half // STEPS
        is_key = (key_ids < half) & (key_ids % per_step == per_step - 1)
        seen = key_ids // per_step <= row_ids % half // per_step
        scores.append(jnp.where(is_key & seen, own_scores, LOW_SCORE))
        own_values = slab[:, HD:].astype(jnp.bfloat16)
        values.append(jnp.concatenate([own_values, own_values], axis=0))
        top = scores[0].max(axis=1, keepdims=True)
        for score in scores[1:]:
            top = jnp.maximum(top, score.max(axis=1, keepdims=True))
        total = jnp.zeros((rows, 1), jnp.float32)
        mixed = jnp.zeros((rows, HD), jnp.float32)
        for score, value in zip(scores, values):
            weight = jnp.exp2((score - top) * EXP_SCALE)
            total = total + weight.sum(axis=1, keepdims=True)
            coarse = weight.astype(jnp.bfloat16)
            fine = (weight - coarse.astype(jnp.float32)).astype(jnp.bfloat16)
            mixed = mixed + dot_nn(coarse, value) + dot_nn(fine, value)
        mixed = mixed / total
        out_ref[req * half : (req + 1) * half, :HD] = mixed[:half].astype(jnp.bfloat16)
        out_ref[req * half : (req + 1) * half, HD:] = mixed[half:].astype(jnp.bfloat16)


def decode_part(got, held, prefix, keyvals, owners, fills, lives):
    reqs = prefix.shape[0]
    blocks = [got, prefix, *keyvals]
    slab = reqs * STEPS * (GROUP // 2 + 1)
    return pl.pallas_call(
        functools.partial(decode_kernel, len(keyvals), held),
        out_shape=jax.ShapeDtypeStruct((slab, got.shape[2]), jnp.bfloat16),
        grid_spec=pltpu.PrefetchScalarGridSpec(
            num_scalar_prefetch=3,
            grid=(1,),
            in_specs=[pl.BlockSpec(memory_space=pltpu.VMEM) for _ in blocks],
            out_specs=pl.BlockSpec(memory_space=pltpu.VMEM),
        ),
        compiler_params=pltpu.CompilerParams(
            dimension_semantics=("arbitrary",), vmem_limit_bytes=16 * MIB
        ),
        cost_estimate=pl.CostEstimate(
            flops=6 * slab * HD * 1536,
            bytes_accessed=2 * reqs * 1536 * 2 * HD,
            transcendentals=slab * 1536,
        ),
        name="decode",
    )(owners, fills, lives, *blocks)


def local(prompt, dec_tokens, w_query, w_keyval, prefix_cache, prompt_len, fill_len, owner):
    replicas = lax.axis_size("replica")
    tensors = lax.axis_size("tensor")
    ring = tensors // 2
    replica_id = lax.axis_index("replica")
    tensor_id = lax.axis_index("tensor")
    per_rep, ctx_len, pair_cols = prefix_cache.shape
    new_len = prompt.shape[0] // per_rep
    depth = prompt.shape[1]
    q_cols = w_query.shape[1]
    half = new_len // 2
    request_count = per_rep * replicas
    first_req = replica_id * per_rep

    def moved(plane, shift):
        return [
            (p * ring + y, ((p + plane) % 2) * ring + (y + shift) % ring)
            for p in range(2)
            for y in range(ring)
        ]

    def send(x, plane, shift):
        return lax.ppermute(x, "tensor", moved(plane, shift))

    my_plane, my_y = tensor_id // ring, tensor_id % ring

    def block_id(plane, shift):
        return ((my_plane + plane) % 2) * ring + (my_y + shift + ring) % ring

    ids = jnp.stack(
        [
            block_id(0, 0),
            block_id(1, 0),
            block_id(0, -1),
            block_id(0, 1),
            block_id(0, 2),
            block_id(1, -1),
            block_id(1, 1),
            block_id(1, 2),
        ]
    ).astype(jnp.int32)

    slot_ids = jnp.arange(request_count, dtype=jnp.int32)
    source = jnp.sum(jnp.where(owner[None, :] == slot_ids[:, None], slot_ids[None, :], 0), axis=1)
    fills = lax.dynamic_slice_in_dim(fill_len, first_req, per_rep, 0)
    lives = lax.dynamic_slice_in_dim(prompt_len, first_req, per_rep, 0)
    my_owner = lax.dynamic_slice_in_dim(owner, first_req, per_rep, 0)
    my_source = lax.dynamic_slice_in_dim(source, first_req, per_rep, 0)

    def exchange(x):
        return lax.all_to_all(x, "replica", split_axis=0, concat_axis=0, tiled=True)

    def zero_dead(x, first_pos, counts):
        pos = first_pos + jnp.arange(x.shape[1], dtype=jnp.int32)
        return jnp.where((pos[None, :] < counts[:, None])[:, :, None], x, jnp.zeros((), x.dtype))

    def for_spread(x):
        block = x.shape[1] // replicas
        return x.reshape(per_rep, replicas, block, pair_cols).transpose(1, 0, 2, 3).reshape(
            replicas, per_rep * block, pair_cols
        )

    def settled(x):
        block = x.shape[1] // per_rep
        return x.reshape(replicas, per_rep, block, pair_cols).transpose(1, 0, 2, 3).reshape(
            per_rep, replicas * block, pair_cols
        )

    rows = per_rep * half
    both = [w_query, w_keyval]
    block = half // replicas
    held = per_rep * block
    dec_pad = jnp.pad(dec_tokens, ((0, DEC_ROWS - dec_tokens.shape[0]), (0, 0)))
    by_req = prompt.reshape(per_rep, 2, half, depth)
    first = jnp.concatenate([by_req[:, 0].reshape(rows, depth), dec_pad], axis=0)
    second = by_req[:, 1].reshape(rows, depth)

    up0, down0, across0 = send(first, 0, 1), send(first, 0, -1), send(first, 1, 0)
    up1, down1, across1 = send(second, 0, 1), send(second, 0, -1), send(second, 1, 0)
    prefix_sent = for_spread(zero_dead(prefix_cache, 0, fills))
    up0, down0, across0, up1, down1, across1, prefix_sent = phase_end(
        up0, down0, across0, up1, down1, across1, prefix_sent
    )

    far0 = send(up0, 0, 1)
    far1 = send(down1, 0, -1)
    prefix_got = exchange(prefix_sent)
    early0 = project(
        [[first], [across0], [up0], [down0]], ids[:4], both, out_type=jnp.float32
    )[0]
    far0, far1, across0, across1, early0 = phase_end(far0, far1, across0, across1, early0)

    across_up0, across_down0 = send(across0, 0, 1), send(across0, 0, -1)
    across_far0 = send(far0, 1, 0)
    early1 = project(
        [[second], [across1], [up1], [down1]], ids[:4], both, out_type=jnp.float32
    )[0]
    prefix_sent = route([prefix_got], source, ctx_len // replicas)
    across_up0, across_down0, across_far0, across1, far1, prefix_sent, early1 = phase_end(
        across_up0, across_down0, across_far0, across1, far1, prefix_sent, early1
    )

    across_up1, across_down1 = send(across1, 0, 1), send(across1, 0, -1)
    across_far1 = send(far1, 1, 0)
    q0, kv0 = project(
        [[far0], [across_up0], [across_down0], [across_far0]], ids[4:], both, start=early0
    )
    got0 = exchange(pack(kv0, per_rep, 0, lives, replicas, q0))
    out0 = prefill_part(0, 2, q0, prefix_cache, [kv0], fills, lives, None)
    prefix_home = settled(exchange(prefix_sent))
    earlier = jnp.pad(prefix_home, ((0, 0), (0, new_len), (0, 0)))
    across_up1, across_down1, across_far1, got0, out0, kv0, earlier = phase_end(
        across_up1, across_down1, across_far1, got0, out0, kv0, earlier
    )

    late1 = [[far1], [across_up1], [across_down1], [across_far1]]
    kv1 = project(late1, ids[4:], [w_keyval], start=early1, start_col=q_cols)[0]
    got1 = exchange(pack(kv1, per_rep, half, lives, replicas))
    dec_back = decode_part(got0, held, prefix_cache, [kv0, kv1], my_owner, fills, lives)
    home = exchange(route([got0, got1], source, block, dec_back))
    decode_cache, decode_out = finish(home, earlier, my_source, block, 2, q_cols)

    q1 = project(late1, ids[4:], [w_query], start=early1)[0]
    prefill_out = prefill_part(1, 2, q1, prefix_cache, [kv0, kv1], fills, lives, out0)
    return (prefill_out, decode_out, decode_cache)


def solution(mesh):
    in_specs = (
        P("replica", "tensor"),
        P("replica", "tensor"),
        P(None, "tensor"),
        P(None, "tensor"),
        P("replica", None, "tensor"),
        P(),
        P(),
        P(),
    )
    out_specs = (P("replica", "tensor"), P("replica", "tensor"), P("replica", None, "tensor"))
    return jax.shard_map(local, mesh=mesh, in_specs=in_specs, out_specs=out_specs, check_vma=False)
```

time: 320 us -> 178 us (0.56)
  matrix products: 79 us -> 0 us
  waiting for transfers between devices: 107 us -> 44.8 us
  Pallas kernels: 0 us -> 54.8 us
  starting transfers between devices: 11.2 us -> 50.5 us
  blocking collectives: 30.3 us -> 0 us
  other arithmetic: 31.2 us -> 1.73 us
  local copies, waits for them, and re-layouts: 43.9 us -> 23.9 us
  between operations: 14.4 us -> 0.92 us
    all_gather x1 -> x0, waiting for transfers between devices: 107 us -> none  [local(): tok_piece = lax.all_gather(prompt, 'tensor', axis=1, tiled=True)]
    dot_general x32 -> x0, matrix products: 79 us -> none  [the longest x12 28.2 us: prompt_head(): jnp.dot(query_rows, key_rows.T, preferred_element_type=jnp.float32)]
    pallas_call x0 -> x13, Pallas kernels: none -> 54.8 us  [the longest x5 26.7 us: project(): pl.pallas_call(functools.partial(project_kernel, (groups, counts, depth),...]
    ppermute x0 -> x14, waiting for transfers between devices: none -> 39.7 us  [send(): return lax.ppermute(x, 'tensor', moved(plane, shift))]
    all_gather x1 -> x0, blocking collectives: 30.3 us -> none  [local(): dec_piece = lax.all_gather(dec_tokens, 'tensor', axis=1, tiled=True)]
    ppermute x0 -> x14, starting transfers between devices: none -> 23.1 us  [send(): return lax.ppermute(x, 'tensor', moved(plane, shift))]
    reduce_sum x14 -> x0, other arithmetic: 18.3 us -> none  [the longest x12 16.9 us: prompt_head(): row_total = jnp.sum(weights, axis=1, keepdims=True)]
    all_to_all x2 -> x5, starting transfers between devices: 11.2 us -> 27.5 us  [exchange(): return lax.all_to_all(x, 'replica', split_axis=0, concat_axis=0, tiled=True)]
  transfers between devices with their start and end apart: 3 -> 19, of which waited for: 1 -> 8; matrix products, arithmetic and copies ran while one was open for 41% -> 4% of each run, Pallas kernels for 0% -> 26%
where the time goes in v1:
time: 178 us; the launch traced here: 177 us
  Pallas kernels  54.8 us (31%)
  starting transfers between devices  50.5 us (28%)
  waiting for transfers between devices  44.8 us (25%)
  local copies, waits for them, and re-layouts  23.9 us (13%)
    ppermute x14, waiting for transfers between devices, send(): return lax.ppermute(x, 'tensor', moved(plane, shift))  39.7 us
    all_to_all x5, starting transfers between devices, exchange(): return lax.all_to_all(x, 'replica', split_axis=0, concat_axis=0, tiled=True)  27.5 us
    pallas_call x5, Pallas kernels, project(): pl.pallas_call(functools.partial(project_kernel, (groups, counts, depth),...  26.7 us
    ppermute x14, starting transfers between devices, send(): return lax.ppermute(x, 'tensor', moved(plane, shift))  23.1 us
    pallas_call x2, Pallas kernels, prefill_part(): pl.pallas_call(functools.partial(prefill_kernel, part, ctx_len), out_shap...  18.6 us
    unnamed x58, local copies, waits for them, and re-layouts  16.9 us
    all_to_all x5, waiting for transfers between devices, exchange(): return lax.all_to_all(x, 'replica', split_axis=0, concat_axis=0, tiled=True)  5.19 us
    pallas_call x2, Pallas kernels, route(): pl.pallas_call(functools.partial(route_kernel, block, len(got)), out_shap...  3.62 us
  transfers between devices with their start and end apart: 19, of which 8 were waited for; matrix products, arithmetic and copies ran while one was open for 4% of the time, Pallas kernels for 26%

profile of v1, /device:TPU:1, one launch (start us, length us, event | category | flops | bytes accessed | tf_op | source)
XLA Modules:
  0.0 176.7 jit_solution(9251641360160283647)
XLA Ops:
  0.7 2.4 %fusion.2 = (bf16[2,1,256,768]{3,2,1,0:T(8,128)(2,1)}, bf16[2,1,256,768]{3,2,1,0:T(8,128)(2,1)S(1)}) fusion(bf16[2,2,256,768]{3,2,1,0:T(8,128)(2,1)} %bitcast.27), kind=kLoop, calls=%fused_computation.9 | loop fusion | bytes 3145728 | tf_op jit(solution)/shard_map/slice | solution.py:570
  8.9 3.6 %collective-permute-start.2 = (bf16[528,768]{1,0:T(8,128)(2,1)}, bf16[528,768]{1,0:T(8,128)(2,1)}, u32[]{:S(2)}, u32[]{:S(2)}) collective-permute-start(bf16[528,768]{1,0:T(8,128)(2,1)} %fusion.1.refs_0_), channel_id=1, source_target_pairs={{0,4},{1,5},{2,6},{3,7},{4,0},{5,1},{6,2},{7,3},{8,12},{9,13},{10,... | collective-permute-start | bytes 2433032 | tf_op jit(solution)/shard_map/ppermute | solution.py:517
  12.7 11.4 %collective-permute-done.3.refs_2_ = bf16[512,768]{1,0:T(8,128)(2,1)S(1)} collective-permute-done((bf16[512,768]{1,0:T(8,128)(2,1)}, bf16[512,768]{1,0:T(8,128)(2,1)S(1)}, u32[]{:S(2)}, u32[]{:S(2)}) %collective-permute-start.3) | collective-permute-done | bytes 786464 | tf_op jit(solution)/shard_map/ppermute | solution.py:517
  24.1 3.4 %collective-permute-start.5 = (bf16[512,768]{1,0:T(8,128)(2,1)}, bf16[512,768]{1,0:T(8,128)(2,1)}, u32[]{:S(2)}, u32[]{:S(2)}) collective-permute-start(bf16[512,768]{1,0:T(8,128)(2,1)} %bitcast.6.refs_0_), channel_id=1, source_target_pairs={{0,4},{1,5},{2,6},{3,7},{4,0},{5,1},{6,2},{7,3},{8,12},{9,13},{10,... | collective-permute-start | bytes 2359304 | tf_op jit(solution)/shard_map/ppermute | solution.py:517
  29.2 13.8 %collective-permute-done.4.refs_3_ = bf16[512,768]{1,0:T(8,128)(2,1)} collective-permute-done((bf16[512,768]{1,0:T(8,128)(2,1)}, bf16[512,768]{1,0:T(8,128)(2,1)}, u32[]{:S(2)}, u32[]{:S(2)}) %collective-permute-start.4) | collective-permute-done | bytes 786464 | tf_op jit(solution)/shard_map/ppermute | solution.py:517
  43.0 3.5 %collective-permute-done.5.refs_1_ = bf16[512,768]{1,0:T(8,128)(2,1)} collective-permute-done((bf16[512,768]{1,0:T(8,128)(2,1)}, bf16[512,768]{1,0:T(8,128)(2,1)}, u32[]{:S(2)}, u32[]{:S(2)}) %collective-permute-start.5) | collective-permute-done | bytes 786464 | tf_op jit(solution)/shard_map/ppermute | solution.py:517
  46.7 2.6 %collective-permute-start.7 = (bf16[512,768]{1,0:T(8,128)(2,1)}, bf16[512,768]{1,0:T(8,128)(2,1)}, u32[]{:S(2)}, u32[]{:S(2)}) collective-permute-start(bf16[512,768]{1,0:T(8,128)(2,1)} %collective-permute-done.4.refs_3_), channel_id=1, source_target_pairs={{0,3},{1,0},{2,1},{3,2},{4,7},{5,4},{6,5},{7,6},{8,11},{9,8},{10,9... | collective-permute-start | bytes 2359304 | tf_op jit(solution)/shard_map/ppermute | solution.py:517
  49.3 7.7 %all-to-all-start = ((bf16[16,128,256]{2,1,0:T(8,128)(2,1)}), bf16[16,128,256]{2,1,0:T(8,128)(2,1)}, u32[]{:S(2)}, u32[]{:S(2)}) async-start(bf16[16,128,256]{2,1,0:T(8,128)(2,1)} %bitcast.23), calls=%async_computation | async-start | bytes 2097152 | tf_op jit(solution)/shard_map/all_to_all | solution.py:545
  57.1 6.0 %project.5.refs_6_ = f32[528,1024]{1,0:T(8,128)S(1)} custom-call(s32[4]{0:T(128)S(1)} %pad_add_fusion.1.ids, bf16[528,768]{1,0:T(8,128)(2,1)} %fusion.1.refs_0_, bf16[528,768]{1,0:T(8,128)(2,1)} %collective-permute-done.2.refs_1_, bf16[528,768]{1,0:T(8,128)(2,1)} %collective-permute-done.refs_2_, bf16[528,768]{1,0:T(8,128)(2,1)} %collective-permute-done.1.refs_3_, ...), custom_call_target="tpu_custom_call" | custom-call | flops 3321888768 | bytes 11698176 | tf_op jit(solution)/shard_map/project/pallas_call | solution.py:125
  67.9 2.7 %collective-permute-start.9 = (bf16[528,768]{1,0:T(8,128)(2,1)}, bf16[528,768]{1,0:T(8,128)(2,1)}, u32[]{:S(2)}, u32[]{:S(2)}) collective-permute-start(bf16[528,768]{1,0:T(8,128)(2,1)} %collective-permute-done.2.refs_1_), channel_id=1, source_target_pairs={{0,3},{1,0},{2,1},{3,2},{4,7},{5,4},{6,5},{7,6},{8,11},{9,8},{10,9... | collective-permute-start | bytes 2433032 | tf_op jit(solution)/shard_map/ppermute | solution.py:517
  70.7 5.8 %project.6.refs_5_ = f32[512,1024]{1,0:T(8,128)S(1)} custom-call(s32[4]{0:T(128)S(1)} %pad_add_fusion.1.ids, bf16[512,768]{1,0:T(8,128)(2,1)} %bitcast.6.refs_0_, bf16[512,768]{1,0:T(8,128)(2,1)} %collective-permute-done.5.refs_1_, bf16[512,768]{1,0:T(8,128)(2,1)S(1)} %copy-done.24, bf16[512,768]{1,0:T(8,128)(2,1)} %collective-permute-done.4.refs_3_, ...), custom_call_target="tpu_custom_call" | custom-call | flops 3221225472 | bytes 11534336 | tf_op jit(solution)/shard_map/project/pallas_call | solution.py:125
  80.8 9.9 %collective-permute-done.10.refs_3_ = bf16[528,768]{1,0:T(8,128)(2,1)} collective-permute-done((bf16[528,768]{1,0:T(8,128)(2,1)}, bf16[528,768]{1,0:T(8,128)(2,1)}, u32[]{:S(2)}, u32[]{:S(2)}) %collective-permute-start.10) | collective-permute-done | bytes 811040 | tf_op jit(solution)/shard_map/ppermute | solution.py:517
  90.7 5.7 %all-to-all-start.2 = ((bf16[16,128,256]{2,1,0:T(8,128)(2,1)}), bf16[16,128,256]{2,1,0:T(8,128)(2,1)}, u32[]{:S(2)}, u32[]{:S(2)}) async-start(bf16[16,128,256]{2,1,0:T(8,128)(2,1)} %copy-done.6), calls=%async_computation.2 | async-start | bytes 2097152 | tf_op jit(solution)/shard_map/all_to_all | solution.py:545
  96.5 2.7 %collective-permute-start.12 = (bf16[512,768]{1,0:T(8,128)(2,1)}, bf16[512,768]{1,0:T(8,128)(2,1)}, u32[]{:S(2)}, u32[]{:S(2)}) collective-permute-start(bf16[512,768]{1,0:T(8,128)(2,1)} %collective-permute-done.5.refs_1_), channel_id=1, source_target_pairs={{0,3},{1,0},{2,1},{3,2},{4,7},{5,4},{6,5},{7,6},{8,11},{9,8},{10,9... | collective-permute-start | bytes 2359304 | tf_op jit(solution)/shard_map/ppermute | solution.py:517
  101.5 6.1 %project.7 = (bf16[528,768]{1,0:T(8,128)(2,1)S(1)}, bf16[528,256]{1,0:T(8,128)(2,1)S(1)}) custom-call(s32[4]{0:T(128)S(1)} %pad_add_fusion.ids, bf16[528,768]{1,0:T(8,128)(2,1)} %collective-permute-done.6.refs_0_, bf16[528,768]{1,0:T(8,128)(2,1)} %collective-permute-done.8.refs_1_, bf16[528,768]{1,0:T(8,128)(2,1)} %collective-permute-done.9.refs_2_, ...), custom_call_target="tpu_custom_call" | custom-call | flops 3321888768 | bytes 11698176 | tf_op jit(solution)/shard_map/project/pallas_call | solution.py:125
  112.3 4.2 %all-to-all-start.1 = ((bf16[16,48,256]{2,1,0:T(8,128)(2,1)}), bf16[16,48,256]{2,1,0:T(8,128)(2,1)S(1)}, u32[]{:S(2)}, u32[]{:S(2)}) async-start(bf16[16,48,256]{2,1,0:T(8,128)(2,1)} %copy-done.14), calls=%async_computation.1 | async-start | bytes 786432 | tf_op jit(solution)/shard_map/all_to_all | solution.py:545
  119.9 8.7 %prefill.2.refs_2_ = bf16[1024,768]{1,0:T(8,128)(2,1)} custom-call(s32[2]{0:T(128)S(1)} %dynamic_slice.12.fill_ref, s32[2]{0:T(128)S(1)} %dynamic_slice.13.live_ref, bf16[528,768]{1,0:T(8,128)(2,1)S(1)} %copy-done.22, bf16[2,1024,256]{2,1,0:T(8,128)(2,1)S(1)} %copy-done.8, bf16[528,256]{1,0:T(8,128)(2,1)S(1)} %copy-done.16), custom_call_target="tpu_custom_call" | custom-call | flops 2013265920 | bytes 2621440 | tf_op jit(solution)/shard_map/prefill/pallas_call | solution.py:396
  132.9 3.9 %project.9.refs_1_.kv_ref = bf16[512,256]{1,0:T(8,128)(2,1)S(1)} custom-call(s32[4]{0:T(128)S(1)} %pad_add_fusion.ids, bf16[512,768]{1,0:T(8,128)(2,1)} %collective-permute-done.7.refs_0_, bf16[512,768]{1,0:T(8,128)(2,1)} %collective-permute-done.11.refs_1_, bf16[512,768]{1,0:T(8,128)(2,1)} %collective-permute-done.12.refs_2_, ...), custom_call_target="tpu_custom_call" | custom-call | flops 805306368 | bytes 5242880 | tf_op jit(solution)/shard_map/project/pallas_call | solution.py:125
  138.8 5.4 %all-to-all-start.3 = ((bf16[16,32,256]{2,1,0:T(8,128)(2,1)}), bf16[16,32,256]{2,1,0:T(8,128)(2,1)S(1)}, u32[]{:S(2)}, u32[]{:S(2)}) async-start(bf16[16,32,256]{2,1,0:T(8,128)(2,1)} %pack.3), calls=%async_computation.3 | async-start | bytes 524288 | tf_op jit(solution)/shard_map/all_to_all | solution.py:545
  148.3 3.3 %all-to-all-done.3.refs_1_ = bf16[16,32,256]{2,1,0:T(8,128)(2,1)S(1)} async-done(((bf16[16,32,256]{2,1,0:T(8,128)(2,1)}), bf16[16,32,256]{2,1,0:T(8,128)(2,1)S(1)}, u32[]{:S(2)}, u32[]{:S(2)}) %all-to-all-start.3) | async-done | bytes 262176 | tf_op jit(solution)/shard_map/all_to_all | solution.py:545
  154.9 4.4 %all-to-all-start.4 = ((bf16[16,80,256]{2,1,0:T(8,128)(2,1)}), bf16[16,80,256]{2,1,0:T(8,128)(2,1)}, u32[]{:S(2)}, u32[]{:S(2)}) async-start(bf16[16,80,256]{2,1,0:T(8,128)(2,1)} %route.3), calls=%async_computation.4 | async-start | bytes 1310720 | tf_op jit(solution)/shard_map/all_to_all | solution.py:545
  159.4 4.9 %project.8.q_ref = bf16[512,768]{1,0:T(8,128)(2,1)S(1)} custom-call(s32[4]{0:T(128)S(1)} %pad_add_fusion.ids, bf16[512,768]{1,0:T(8,128)(2,1)} %collective-permute-done.7.refs_0_, bf16[512,768]{1,0:T(8,128)(2,1)} %collective-permute-done.11.refs_1_, bf16[512,768]{1,0:T(8,128)(2,1)} %collective-permute-done.12.refs_2_, ...), custom_call_target="tpu_custom_call" | custom-call | flops 2415919104 | bytes 9437184 | tf_op jit(solution)/shard_map/project/pallas_call | solution.py:125
  164.3 9.9 %prefill.3 = bf16[1024,768]{1,0:T(8,128)(2,1)} custom-call(s32[2]{0:T(128)S(1)} %dynamic_slice.12.fill_ref, s32[2]{0:T(128)S(1)} %dynamic_slice.13.live_ref, bf16[512,768]{1,0:T(8,128)(2,1)S(1)} %project.8.q_ref, bf16[2,1024,256]{2,1,0:T(8,128)(2,1)S(1)} %copy-done.10, bf16[528,256]{1,0:T(8,128)(2,1)S(1)} %copy-done.18, ...), custom_call_target="tpu_custom_call", output_to_operand_aliasing={{}: (6, {})} | custom-call | flops 2013265920 | bytes 2621440 | tf_op jit(solution)/shard_map/prefill/pallas_call | solution.py:396
  174.2 2.5 %finish.1 = (bf16[2,1536,256]{2,1,0:T(8,128)(2,1)}, bf16[4,768]{1,0:T(4,128)(2,1)}) custom-call(s32[2]{0:T(128)S(1)} %dynamic_slice.14.source, bf16[16,80,256]{2,1,0:T(8,128)(2,1)} %all-to-all-done.4.home_ref, bf16[2,1536,256]{2,1,0:T(8,128)(2,1)} %pad.9.earlier_ref), custom_call_target="tpu_custom_call", output_to_operand_aliasing={{0}: (2, {})} | custom-call | tf_op jit(solution)/shard_map/finish/pallas_call | solution.py:283
  (99 shorter events, 41.2 us)
Async XLA Ops:
  0.6 26.9 %copy-start.26 = (s32[32]{0:T(128)S(1)}, s32[32]{0:T(128)}, u32[]{:S(2)}) copy-start(s32[32]{0:T(128)} %param.14) | copy-start | bytes 388
  0.7 27.0 %copy-start.7 = (bf16[2,1024,256]{2,1,0:T(8,128)(2,1)S(1)}, bf16[2,1024,256]{2,1,0:T(8,128)(2,1)}, u32[]{:S(2)}) copy-start(bf16[2,1024,256]{2,1,0:T(8,128)(2,1)} %prefix_ref.5) | copy-start | bytes 3145732
  3.1 21.0 %collective-permute-start.3 = (bf16[512,768]{1,0:T(8,128)(2,1)}, bf16[512,768]{1,0:T(8,128)(2,1)S(1)}, u32[]{:S(2)}, u32[]{:S(2)}) collective-permute-start(bf16[512,768]{1,0:T(8,128)(2,1)} %bitcast.6.refs_0_), channel_id=1, source_target_pairs={{0,1},{1,2},{2,3},{3,0},{4,5},{5,6},{6,7},{7,4},{8,9},{9,10},{10,1... | collective-permute-start | bytes 2359304 | tf_op jit(solution)/shard_map/ppermute | solution.py:517
  6.2 40.3 %collective-permute-start = (bf16[528,768]{1,0:T(8,128)(2,1)}, bf16[528,768]{1,0:T(8,128)(2,1)}, u32[]{:S(2)}, u32[]{:S(2)}) collective-permute-start(bf16[528,768]{1,0:T(8,128)(2,1)} %fusion.1.refs_0_), channel_id=1, source_target_pairs={{0,1},{1,2},{2,3},{3,0},{4,5},{5,6},{6,7},{7,4},{8,9},{9,10},{10,1... | collective-permute-start | bytes 2433032 | tf_op jit(solution)/shard_map/ppermute | solution.py:517
  7.5 39.0 %collective-permute-start.1 = (bf16[528,768]{1,0:T(8,128)(2,1)}, bf16[528,768]{1,0:T(8,128)(2,1)}, u32[]{:S(2)}, u32[]{:S(2)}) collective-permute-start(bf16[528,768]{1,0:T(8,128)(2,1)} %fusion.1.refs_0_), channel_id=1, source_target_pairs={{0,3},{1,0},{2,1},{3,2},{4,7},{5,4},{6,5},{7,6},{8,11},{9,8},{10,9... | collective-permute-start | bytes 2433032 | tf_op jit(solution)/shard_map/ppermute | solution.py:517
  8.9 37.7 %collective-permute-start.2 = (bf16[528,768]{1,0:T(8,128)(2,1)}, bf16[528,768]{1,0:T(8,128)(2,1)}, u32[]{:S(2)}, u32[]{:S(2)}) collective-permute-start(bf16[528,768]{1,0:T(8,128)(2,1)} %fusion.1.refs_0_), channel_id=1, source_target_pairs={{0,4},{1,5},{2,6},{3,7},{4,0},{5,1},{6,2},{7,3},{8,12},{9,13},{10,... | collective-permute-start | bytes 2433032 | tf_op jit(solution)/shard_map/ppermute | solution.py:517
  12.4 30.5 %collective-permute-start.4 = (bf16[512,768]{1,0:T(8,128)(2,1)}, bf16[512,768]{1,0:T(8,128)(2,1)}, u32[]{:S(2)}, u32[]{:S(2)}) collective-permute-start(bf16[512,768]{1,0:T(8,128)(2,1)} %bitcast.6.refs_0_), channel_id=1, source_target_pairs={{0,3},{1,0},{2,1},{3,2},{4,7},{5,4},{6,5},{7,6},{8,11},{9,8},{10,9... | collective-permute-start | bytes 2359304 | tf_op jit(solution)/shard_map/ppermute | solution.py:517
  24.1 22.4 %collective-permute-start.5 = (bf16[512,768]{1,0:T(8,128)(2,1)}, bf16[512,768]{1,0:T(8,128)(2,1)}, u32[]{:S(2)}, u32[]{:S(2)}) collective-permute-start(bf16[512,768]{1,0:T(8,128)(2,1)} %bitcast.6.refs_0_), channel_id=1, source_target_pairs={{0,4},{1,5},{2,6},{3,7},{4,0},{5,1},{6,2},{7,3},{8,12},{9,13},{10,... | collective-permute-start | bytes 2359304 | tf_op jit(solution)/shard_map/ppermute | solution.py:517
  28.1 29.0 %copy-start = (bf16[6144,256]{1,0:T(8,128)(2,1)S(1)}, bf16[6144,256]{1,0:T(8,128)(2,1)}, u32[]{:S(2)}) copy-start(bf16[6144,256]{1,0:T(8,128)(2,1)} %refs_4_.9) | copy-start | bytes 9437188
  46.5 19.0 %collective-permute-start.6 = (bf16[528,768]{1,0:T(8,128)(2,1)}, bf16[528,768]{1,0:T(8,128)(2,1)}, u32[]{:S(2)}, u32[]{:S(2)}) collective-permute-start(bf16[528,768]{1,0:T(8,128)(2,1)} %collective-permute-done.refs_2_), channel_id=1, source_target_pairs={{0,1},{1,2},{2,3},{3,0},{4,5},{5,6},{6,7},{7,4},{8,9},{9,10},{10,1... | collective-permute-start | bytes 2433032 | tf_op jit(solution)/shard_map/ppermute | solution.py:517
  46.7 17.9 %collective-permute-start.7 = (bf16[512,768]{1,0:T(8,128)(2,1)}, bf16[512,768]{1,0:T(8,128)(2,1)}, u32[]{:S(2)}, u32[]{:S(2)}) collective-permute-start(bf16[512,768]{1,0:T(8,128)(2,1)} %collective-permute-done.4.refs_3_), channel_id=1, source_target_pairs={{0,3},{1,0},{2,1},{3,2},{4,7},{5,4},{6,5},{7,6},{8,11},{9,8},{10,9... | collective-permute-start | bytes 2359304 | tf_op jit(solution)/shard_map/ppermute | solution.py:517
  49.3 28.5 %all-to-all-start = ((bf16[16,128,256]{2,1,0:T(8,128)(2,1)}), bf16[16,128,256]{2,1,0:T(8,128)(2,1)}, u32[]{:S(2)}, u32[]{:S(2)}) async-start(bf16[16,128,256]{2,1,0:T(8,128)(2,1)} %bitcast.23), calls=%async_computation | async-start | bytes 2097152 | tf_op jit(solution)/shard_map/all_to_all | solution.py:545
  57.1 13.6 %copy-start.24 = (bf16[512,768]{1,0:T(8,128)(2,1)S(1)}, bf16[512,768]{1,0:T(8,128)(2,1)}, u32[]{:S(2)}) copy-start(bf16[512,768]{1,0:T(8,128)(2,1)} %copy-done.23) | copy-start | bytes 2359300
  65.5 25.2 %collective-permute-start.10 = (bf16[528,768]{1,0:T(8,128)(2,1)}, bf16[528,768]{1,0:T(8,128)(2,1)}, u32[]{:S(2)}, u32[]{:S(2)}) collective-permute-start(bf16[528,768]{1,0:T(8,128)(2,1)} %collective-permute-done.6.refs_0_), channel_id=1, source_target_pairs={{0,4},{1,5},{2,6},{3,7},{4,0},{5,1},{6,2},{7,3},{8,12},{9,13},{10,... | collective-permute-start | bytes 2433032 | tf_op jit(solution)/shard_map/ppermute | solution.py:517
  67.9 22.8 %collective-permute-start.8 = (bf16[528,768]{1,0:T(8,128)(2,1)}, bf16[528,768]{1,0:T(8,128)(2,1)}, u32[]{:S(2)}, u32[]{:S(2)}) collective-permute-start(bf16[528,768]{1,0:T(8,128)(2,1)} %collective-permute-done.2.refs_1_), channel_id=1, source_target_pairs={{0,1},{1,2},{2,3},{3,0},{4,5},{5,6},{6,7},{7,4},{8,9},{9,10},{10,1... | collective-permute-start | bytes 2433032 | tf_op jit(solution)/shard_map/ppermute | solution.py:517
  67.9 22.8 %collective-permute-start.9 = (bf16[528,768]{1,0:T(8,128)(2,1)}, bf16[528,768]{1,0:T(8,128)(2,1)}, u32[]{:S(2)}, u32[]{:S(2)}) collective-permute-start(bf16[528,768]{1,0:T(8,128)(2,1)} %collective-permute-done.2.refs_1_), channel_id=1, source_target_pairs={{0,3},{1,0},{2,1},{3,2},{4,7},{5,4},{6,5},{7,6},{8,11},{9,8},{10,9... | collective-permute-start | bytes 2433032 | tf_op jit(solution)/shard_map/ppermute | solution.py:517
  77.8 18.6 %copy-start.27 = (s32[32]{0:T(128)S(1)}, s32[32]{0:T(128)}, u32[]{:S(2)}) copy-start(s32[32]{0:T(128)} %param.13) | copy-start | bytes 388
  90.7 21.6 %all-to-all-start.2 = ((bf16[16,128,256]{2,1,0:T(8,128)(2,1)}), bf16[16,128,256]{2,1,0:T(8,128)(2,1)}, u32[]{:S(2)}, u32[]{:S(2)}) async-start(bf16[16,128,256]{2,1,0:T(8,128)(2,1)} %copy-done.6), calls=%async_computation.2 | async-start | bytes 2097152 | tf_op jit(solution)/shard_map/all_to_all | solution.py:545
  96.5 34.8 %collective-permute-start.11 = (bf16[512,768]{1,0:T(8,128)(2,1)}, bf16[512,768]{1,0:T(8,128)(2,1)}, u32[]{:S(2)}, u32[]{:S(2)}) collective-permute-start(bf16[512,768]{1,0:T(8,128)(2,1)} %collective-permute-done.5.refs_1_), channel_id=1, source_target_pairs={{0,1},{1,2},{2,3},{3,0},{4,5},{5,6},{6,7},{7,4},{8,9},{9,10},{10,1... | collective-permute-start | bytes 2359304 | tf_op jit(solution)/shard_map/ppermute | solution.py:517
  96.5 34.8 %collective-permute-start.12 = (bf16[512,768]{1,0:T(8,128)(2,1)}, bf16[512,768]{1,0:T(8,128)(2,1)}, u32[]{:S(2)}, u32[]{:S(2)}) collective-permute-start(bf16[512,768]{1,0:T(8,128)(2,1)} %collective-permute-done.5.refs_1_), channel_id=1, source_target_pairs={{0,3},{1,0},{2,1},{3,2},{4,7},{5,4},{6,5},{7,6},{8,11},{9,8},{10,9... | collective-permute-start | bytes 2359304 | tf_op jit(solution)/shard_map/ppermute | solution.py:517
  99.2 32.1 %collective-permute-start.13 = (bf16[512,768]{1,0:T(8,128)(2,1)}, bf16[512,768]{1,0:T(8,128)(2,1)}, u32[]{:S(2)}, u32[]{:S(2)}) collective-permute-start(bf16[512,768]{1,0:T(8,128)(2,1)} %collective-permute-done.7.refs_0_), channel_id=1, source_target_pairs={{0,4},{1,5},{2,6},{3,7},{4,0},{5,1},{6,2},{7,3},{8,12},{9,13},{10,... | collective-permute-start | bytes 2359304 | tf_op jit(solution)/shard_map/ppermute | solution.py:517
  112.3 19.0 %all-to-all-start.1 = ((bf16[16,48,256]{2,1,0:T(8,128)(2,1)}), bf16[16,48,256]{2,1,0:T(8,128)(2,1)S(1)}, u32[]{:S(2)}, u32[]{:S(2)}) async-start(bf16[16,48,256]{2,1,0:T(8,128)(2,1)} %copy-done.14), calls=%async_computation.1 | async-start | bytes 786432 | tf_op jit(solution)/shard_map/all_to_all | solution.py:545
  138.8 12.8 %all-to-all-start.3 = ((bf16[16,32,256]{2,1,0:T(8,128)(2,1)}), bf16[16,32,256]{2,1,0:T(8,128)(2,1)S(1)}, u32[]{:S(2)}, u32[]{:S(2)}) async-start(bf16[16,32,256]{2,1,0:T(8,128)(2,1)} %pack.3), calls=%async_computation.3 | async-start | bytes 524288 | tf_op jit(solution)/shard_map/all_to_all | solution.py:545
  154.9 19.3 %all-to-all-start.4 = ((bf16[16,80,256]{2,1,0:T(8,128)(2,1)}), bf16[16,80,256]{2,1,0:T(8,128)(2,1)}, u32[]{:S(2)}, u32[]{:S(2)}) async-start(bf16[16,80,256]{2,1,0:T(8,128)(2,1)} %route.3), calls=%async_computation.4 | async-start | bytes 1310720 | tf_op jit(solution)/shard_map/all_to_all | solution.py:545
  (24 other events, 73.0 us)

commit v2 on v1

--- a/solution.py
+++ b/solution.py
@@ -15,7 +15,8 @@
 STEPS = 2
 DEC_ROWS = 16
 KEY_BLOCK = 256
-MIB = 1024 * 1024
+SMALL_VMEM = 16 * 1024 * 1024
+WHOLE_VMEM = 62 * 1024 * 1024
 
 LOW_SCORE = -1e30
 EXP_SCALE = math.log2(math.e) / math.sqrt(HD)
@@ -39,7 +40,7 @@
     return tiles
 
 
-def project_kernel(shape, has_start, widths, ids, *refs):
+def project_kernel(shape, has_start, start_col, spread, widths, ids, lives, *refs):
     groups, counts, depth = shape
     refs = list(refs)
     pieces = [[refs.pop(0) for _ in counts] for _ in range(groups)]
@@ -73,22 +74,29 @@
         ]
 
     steps = groups // per
-    for k in range(steps):
+    all_columns = sum(widths)
+    for copy in copies(0):
+        copy.start()
+    if has_start:
+        before = pltpu.make_async_copy(
+            start_ref.at[:, pl.ds(start_col, all_columns)], total, sems.at[steps, 0]
+        )
+        before.start()
+    for k in range(1, steps):
         for copy in copies(k):
             copy.start()
-    all_columns = sum(widths)
     for k in range(steps):
         for copy in copies(k):
             copy.wait()
+        if k == 0 and has_start:
+            before.wait()
         for row, count in row_tiles(counts):
             for col in range(0, all_columns, 512):
                 width = min(512, all_columns - col)
                 at = (slice(row, row + count), slice(col, col + width))
                 part = dot_nn(held[k, row : row + count, :], weight_held[k, :, col : col + width])
-                if k:
+                if k or has_start:
                     part = part + total[at]
-                elif has_start:
-                    part = part + start_ref[row : row + count, col : col + width]
                 if k < steps - 1:
                     total[at] = part
                     continue
@@ -97,14 +105,44 @@
                     low = row - offsets[group]
                     outs[group][low : low + count, col : col + width] = part
                     continue
-                for out, first, wide in zip(outs, columns, widths):
+                for out, first, wide in zip(outs[: len(widths)], columns, widths):
                     low, high = max(first, col), min(first + wide, col + width)
                     if low < high:
                         value = part[:, low - col : high - col].astype(jnp.bfloat16)
                         out[row : row + count, low - first : high - first] = value
-
-
-def project(pieces, ids, weights, start=None, start_col=0, out_type=jnp.bfloat16):
+    if spread:
+        pack(spread, lives, outs)
+
+
+def pack(spread, lives, outs):
+    reqs, first_pos, dests, _ = spread
+    q_ref, kv_ref, spread_ref = outs[0], outs[-2], outs[-1]
+    columns = kv_ref.shape[1]
+    each = kv_ref.shape[0] // reqs // 16 * 16
+    block = each // dests
+    pos = first_pos + lax.broadcasted_iota(jnp.int32, (each, 1), 0)
+    for req in range(reqs):
+        rows = kv_ref[req * each : (req + 1) * each, :]
+        rows = jnp.where(pos < lives[req], rows, jnp.zeros_like(rows))
+        for dest in range(dests):
+            spread_ref[dest, req * block : (req + 1) * block, :] = rows[
+                dest * block : (dest + 1) * block
+            ]
+    if spread_ref.shape[1] == reqs * block:
+        return
+    queries = q_ref[reqs * each :, :].astype(jnp.float32)
+    keyvals = kv_ref[reqs * each :, :].astype(jnp.float32)
+    slab = []
+    for row in range(reqs * STEPS):
+        for low in range(0, queries.shape[1], columns):
+            slab.append(queries[row : row + 1, low : low + columns])
+        slab.append(keyvals[row : row + 1, :])
+    slab = jnp.concatenate(slab, axis=0).astype(jnp.bfloat16)
+    for dest in range(dests):
+        spread_ref[dest, reqs * block :, :] = slab
+
+
+def project(pieces, ids, weights, lives, start=None, start_col=0, out_type=jnp.bfloat16, spread=None):
     groups = len(pieces)
     counts = tuple(x.shape[0] for x in pieces[0])
     depth = pieces[0][0].shape[1]
@@ -114,21 +152,27 @@
     operands = [x for group in pieces for x in group] + list(weights)
     in_specs = [pl.BlockSpec(memory_space=pltpu.HBM)] * len(operands)
     if has_start:
-        in_specs.append(pl.BlockSpec((rows, columns), lambda *_: (0, start_col // columns)))
+        in_specs.append(pl.BlockSpec(memory_space=pltpu.HBM))
         operands.append(start)
     if out_type == jnp.float32:
         out_shape = [jax.ShapeDtypeStruct((count, columns), jnp.float32) for count in counts]
     else:
         out_shape = [jax.ShapeDtypeStruct((rows, w), jnp.bfloat16) for w in widths]
+    if spread:
+        reqs, _, dests, has_dec = spread
+        length = rows // reqs // 16 * 16 * reqs // dests
+        if has_dec:
+            length += reqs * STEPS * (widths[0] // widths[-1] + 1)
+        out_shape.append(jax.ShapeDtypeStruct((dests, length, widths[-1]), jnp.bfloat16))
     per = 1
     copies = per * (len(counts) + 2 * len(widths))
     return pl.pallas_call(
         functools.partial(
-            project_kernel, (groups, counts, depth), has_start, widths
+            project_kernel, (groups, counts, depth), has_start, start_col, spread, widths
         ),
         out_shape=out_shape,
         grid_spec=pltpu.PrefetchScalarGridSpec(
-            num_scalar_prefetch=1,
+            num_scalar_prefetch=2,
             grid=(1,),
             in_specs=in_specs,
             out_specs=[pl.BlockSpec(memory_space=pltpu.VMEM)] * len(out_shape),
@@ -136,11 +180,11 @@
                 pltpu.VMEM((groups // per, rows, per * depth), jnp.bfloat16),
                 pltpu.VMEM((groups // per, per * depth, columns), jnp.bfloat16),
                 pltpu.VMEM((rows, columns), jnp.float32),
-                pltpu.SemaphoreType.DMA((groups // per, copies)),
+                pltpu.SemaphoreType.DMA((groups // per + 1, copies)),
             ],
         ),
         compiler_params=pltpu.CompilerParams(
-            dimension_semantics=("arbitrary",), vmem_limit_bytes=40 * MIB
+            dimension_semantics=("arbitrary",), vmem_limit_bytes=WHOLE_VMEM
         ),
         cost_estimate=pl.CostEstimate(
             flops=2 * rows * depth * groups * columns,
@@ -148,66 +192,7 @@
             transcendentals=0,
         ),
         name="project",
-    )(ids, *operands)
-
-
-def pack_kernel(reqs, first_pos, live_ref, kv_ref, *refs):
-    out_ref = refs[-1]
-    dests, length, columns = out_ref.shape
-    each = kv_ref.shape[0] // reqs // 16 * 16
-    block = each // dests
-    pos = first_pos + lax.broadcasted_iota(jnp.int32, (each, 1), 0)
-    for req in range(reqs):
-        rows = kv_ref[req * each : (req + 1) * each, :]
-        rows = jnp.where(pos < live_ref[req], rows, jnp.zeros_like(rows))
-        for dest in range(dests):
-            out_ref[dest, req * block : (req + 1) * block, :] = rows[
-                dest * block : (dest + 1) * block
-            ]
-    if len(refs) == 1:
-        return
-    q_ref = refs[0]
-    count = length - reqs * block
-    per = q_ref.shape[1] // columns + 1
-    at = reqs * each
-    queries = q_ref[...].astype(jnp.float32)
-    keyvals = kv_ref[at : at + q_ref.shape[0], :].astype(jnp.float32)
-    slab = []
-    for row in range(count // per):
-        for part in range(per - 1):
-            slab.append(queries[row : row + 1, part * columns : (part + 1) * columns])
-        slab.append(keyvals[row : row + 1, :])
-    slab = jnp.concatenate(slab, axis=0).astype(jnp.bfloat16)
-    for dest in range(dests):
-        out_ref[dest, reqs * block :, :] = slab
-
-
-def pack(keyvals, reqs, first_pos, lives, dests, queries=None):
-    columns = keyvals.shape[1]
-    each = keyvals.shape[0] // reqs // 16 * 16
-    length = reqs * each // dests
-    operands = [keyvals]
-    in_specs = [pl.BlockSpec(memory_space=pltpu.VMEM)]
-    if queries is not None:
-        length += reqs * STEPS * (queries.shape[1] // columns + 1)
-        operands.append(queries)
-        row = reqs * each // DEC_ROWS
-        in_specs.append(pl.BlockSpec((DEC_ROWS, queries.shape[1]), lambda *_: (row, 0)))
-    return pl.pallas_call(
-        functools.partial(pack_kernel, reqs, first_pos),
-        out_shape=jax.ShapeDtypeStruct((dests, length, columns), keyvals.dtype),
-        grid_spec=pltpu.PrefetchScalarGridSpec(
-            num_scalar_prefetch=1,
-            grid=(1,),
-            in_specs=in_specs,
-            out_specs=pl.BlockSpec(memory_space=pltpu.VMEM),
-        ),
-        compiler_params=pltpu.CompilerParams(vmem_limit_bytes=16 * MIB),
-        cost_estimate=pl.CostEstimate(
-            flops=0, bytes_accessed=4 * dests * length * columns, transcendentals=0
-        ),
-        name="pack",
-    )(lives, *operands)
+    )(ids, lives, *operands)
 
 
 def route_kernel(block, count, source, *refs):
@@ -242,12 +227,34 @@
             in_specs=[pl.BlockSpec(memory_space=pltpu.VMEM)] * len(operands),
             out_specs=pl.BlockSpec(memory_space=pltpu.VMEM),
         ),
-        compiler_params=pltpu.CompilerParams(vmem_limit_bytes=16 * MIB),
+        compiler_params=pltpu.CompilerParams(vmem_limit_bytes=SMALL_VMEM),
         cost_estimate=pl.CostEstimate(
             flops=0, bytes_accessed=4 * dests * length * columns, transcendentals=0
         ),
         name="route",
     )(source, *operands)
+
+
+def settle_kernel(got_ref, out_ref):
+    dests, length, _ = got_ref.shape
+    block = out_ref.shape[1] // dests
+    at = pl.ds(pl.multiple_of(pl.program_id(0) * block, block), block)
+    for dest in range(dests):
+        out_ref[0, dest * block : (dest + 1) * block, :] = got_ref[dest, at, :]
+
+
+def settle(got, per_rep, total_len):
+    dests, length, columns = got.shape
+    held = dests * length // per_rep
+    return pl.pallas_call(
+        settle_kernel,
+        out_shape=jax.ShapeDtypeStruct((per_rep, total_len, columns), got.dtype),
+        grid=(per_rep,),
+        in_specs=[pl.BlockSpec(memory_space=pltpu.VMEM)],
+        out_specs=pl.BlockSpec((1, held, columns), lambda c: (c, 0, 0)),
+        compiler_params=pltpu.CompilerParams(vmem_limit_bytes=SMALL_VMEM),
+        name="settle",
+    )(got)
 
 
 def finish_kernel(block, count, source, home_ref, earlier_ref, cache_ref, out_ref):
@@ -299,7 +306,7 @@
             ),
         ),
         input_output_aliases={2: 0},
-        compiler_params=pltpu.CompilerParams(vmem_limit_bytes=16 * MIB),
+        compiler_params=pltpu.CompilerParams(vmem_limit_bytes=SMALL_VMEM),
         name="finish",
     )(source, home, earlier)
 
@@ -360,10 +367,10 @@
                 mixed = jnp.where(first_row + row_ids < live, mixed, 0.0)
             out_ref[:, cols] = mixed.astype(jnp.bfloat16)
 
-        @pl.loop(0, GROUP // 2)
-        def _(pair):
-            one_head(2 * pair)
-            one_head(2 * pair + 1)
+        @pl.loop(0, GROUP // 3)
+        def _(triple):
+            for n in range(3):
+                one_head(3 * triple + n)
 
     block_count = (fill + KEY_BLOCK - 1) // KEY_BLOCK
     is_live = first_row < live
@@ -404,7 +411,7 @@
         ),
         input_output_aliases=aliases,
         compiler_params=pltpu.CompilerParams(
-            dimension_semantics=("arbitrary",), vmem_limit_bytes=24 * MIB
+            dimension_semantics=("arbitrary",), vmem_limit_bytes=WHOLE_VMEM
         ),
         cost_estimate=pl.CostEstimate(
             flops=4 * reqs * rows * cols * (ctx_len + rows),
@@ -481,7 +488,7 @@
             out_specs=pl.BlockSpec(memory_space=pltpu.VMEM),
         ),
         compiler_params=pltpu.CompilerParams(
-            dimension_semantics=("arbitrary",), vmem_limit_bytes=16 * MIB
+            dimension_semantics=("arbitrary",), vmem_limit_bytes=WHOLE_VMEM
         ),
         cost_estimate=pl.CostEstimate(
             flops=6 * slab * HD * 1536,
@@ -554,12 +561,6 @@
             replicas, per_rep * block, pair_cols
         )
 
-    def settled(x):
-        block = x.shape[1] // per_rep
-        return x.reshape(replicas, per_rep, block, pair_cols).transpose(1, 0, 2, 3).reshape(
-            per_rep, replicas * block, pair_cols
-        )
-
     rows = per_rep * half
     both = [w_query, w_keyval]
     block = half // replicas
@@ -571,50 +572,63 @@
 
     up0, down0, across0 = send(first, 0, 1), send(first, 0, -1), send(first, 1, 0)
     up1, down1, across1 = send(second, 0, 1), send(second, 0, -1), send(second, 1, 0)
-    prefix_sent = for_spread(zero_dead(prefix_cache, 0, fills))
-    up0, down0, across0, up1, down1, across1, prefix_sent = phase_end(
-        up0, down0, across0, up1, down1, across1, prefix_sent
+    prefix_got = exchange(for_spread(zero_dead(prefix_cache, 0, fills)))
+    prefix_sent = route([prefix_got], source, ctx_len // replicas)
+    early0 = project(
+        [[first], [across0], [up0], [down0]], ids[:4], both, lives, out_type=jnp.float32
+    )[0]
+    up0, down0, across0, up1, down1, across1, prefix_sent, early0 = phase_end(
+        up0, down0, across0, up1, down1, across1, prefix_sent, early0
     )
 
     far0 = send(up0, 0, 1)
     far1 = send(down1, 0, -1)
-    prefix_got = exchange(prefix_sent)
-    early0 = project(
-        [[first], [across0], [up0], [down0]], ids[:4], both, out_type=jnp.float32
-    )[0]
+    prefix_home = exchange(prefix_sent)
     far0, far1, across0, across1, early0 = phase_end(far0, far1, across0, across1, early0)
 
     across_up0, across_down0 = send(across0, 0, 1), send(across0, 0, -1)
     across_far0 = send(far0, 1, 0)
     early1 = project(
-        [[second], [across1], [up1], [down1]], ids[:4], both, out_type=jnp.float32
+        [[second], [across1], [up1], [down1], [far1]], ids[:5], both, lives, out_type=jnp.float32
     )[0]
-    prefix_sent = route([prefix_got], source, ctx_len // replicas)
-    across_up0, across_down0, across_far0, across1, far1, prefix_sent, early1 = phase_end(
-        across_up0, across_down0, across_far0, across1, far1, prefix_sent, early1
+    across_up0, across_down0, across_far0, across1, far1, prefix_home, early1 = phase_end(
+        across_up0, across_down0, across_far0, across1, far1, prefix_home, early1
     )
 
     across_up1, across_down1 = send(across1, 0, 1), send(across1, 0, -1)
     across_far1 = send(far1, 1, 0)
-    q0, kv0 = project(
-        [[far0], [across_up0], [across_down0], [across_far0]], ids[4:], both, start=early0
+    q0, kv0, spread0 = project(
+        [[far0], [across_up0], [across_down0], [across_far0]],
+        ids[4:],
+        both,
+        lives,
+        start=early0,
+        spread=(per_rep, 0, replicas, True),
     )
-    got0 = exchange(pack(kv0, per_rep, 0, lives, replicas, q0))
+    got0 = exchange(spread0)
     out0 = prefill_part(0, 2, q0, prefix_cache, [kv0], fills, lives, None)
-    prefix_home = settled(exchange(prefix_sent))
-    earlier = jnp.pad(prefix_home, ((0, 0), (0, new_len), (0, 0)))
-    across_up1, across_down1, across_far1, got0, out0, kv0, earlier = phase_end(
-        across_up1, across_down1, across_far1, got0, out0, kv0, earlier
+    across_up1, across_down1, across_far1, got0, out0, kv0 = phase_end(
+        across_up1, across_down1, across_far1, got0, out0, kv0
     )
 
-    late1 = [[far1], [across_up1], [across_down1], [across_far1]]
-    kv1 = project(late1, ids[4:], [w_keyval], start=early1, start_col=q_cols)[0]
-    got1 = exchange(pack(kv1, per_rep, half, lives, replicas))
+    late1 = [[across_up1], [across_down1], [across_far1]]
+    kv1, spread1 = project(
+        late1,
+        ids[5:],
+        [w_keyval],
+        lives,
+        start=early1,
+        start_col=q_cols,
+        spread=(per_rep, half, replicas, False),
+    )
+    got1 = exchange(spread1)
+    q1 = project(late1, ids[5:], [w_query], lives, start=early1)[0]
     dec_back = decode_part(got0, held, prefix_cache, [kv0, kv1], my_owner, fills, lives)
+    dec_back, q1 = phase_end(dec_back, q1)
     home = exchange(route([got0, got1], source, block, dec_back))
+    earlier = settle(prefix_home, per_rep, ctx_len + new_len)
     decode_cache, decode_out = finish(home, earlier, my_source, block, 2, q_cols)
 
-    q1 = project(late1, ids[4:], [w_query], start=early1)[0]
     prefill_out = prefill_part(1, 2, q1, prefix_cache, [kv0, kv1], fills, lives, out0)
     return (prefill_out, decode_out, decode_cache)
 

time: 178 us -> 170 us (0.955)
  local copies, waits for them, and re-layouts: 23.9 us -> 5.48 us
  Pallas kernels: 54.8 us -> 65.4 us
  waiting for transfers between devices: 44.8 us -> 39.2 us
  starting transfers between devices: 50.5 us -> 55.4 us
    unnamed x58 -> x18, local copies, waits for them, and re-layouts: 16.9 us -> 0.04 us
    pallas_call x5, Pallas kernels: 26.7 us -> 34.6 us  [project(): pl.pallas_call(functools.partial(project_kernel, (groups, counts, depth),...]
    all_to_all x5, waiting for transfers between devices: 5.19 us -> 0.01 us  [exchange(): return lax.all_to_all(x, 'replica', split_axis=0, concat_axis=0, tiled=True)]
    all_to_all x5, starting transfers between devices: 27.5 us -> 32.2 us  [exchange(): return lax.all_to_all(x, 'replica', split_axis=0, concat_axis=0, tiled=True)]
    pallas_call x2, Pallas kernels: 18.6 us -> 21.3 us  [prefill_part(): pl.pallas_call(functools.partial(prefill_kernel, part, ctx_len), out_shap...]
    pallas_call x1, Pallas kernels: 1.47 us -> 3.68 us  [decode_part(): pl.pallas_call(functools.partial(decode_kernel, len(keyvals), held), out_...]
  transfers between devices with their start and end apart: 19 -> 19, of which waited for: 8 -> 7; matrix products, arithmetic and copies ran while one was open for 4% -> 3% of each run, Pallas kernels for 26% -> 34%
where the time goes in v2:
time: 170 us
  Pallas kernels  65.4 us (38%)
  starting transfers between devices  55.4 us (33%)
  waiting for transfers between devices  39.2 us (23%)
  local copies, waits for them, and re-layouts  5.48 us (3%)
  other arithmetic  3.34 us (2%)
    ppermute x14, waiting for transfers between devices, send(): return lax.ppermute(x, 'tensor', moved(plane, shift))  39.2 us
    pallas_call x5, Pallas kernels, project(): pl.pallas_call(functools.partial(project_kernel, (groups, counts, depth),...  34.6 us
    all_to_all x5, starting transfers between devices, exchange(): return lax.all_to_all(x, 'replica', split_axis=0, concat_axis=0, tiled=True)  32.2 us
    ppermute x14, starting transfers between devices, send(): return lax.ppermute(x, 'tensor', moved(plane, shift))  23.2 us
    pallas_call x2, Pallas kernels, prefill_part(): pl.pallas_call(functools.partial(prefill_kernel, part, ctx_len), out_shap...  21.3 us
    pallas_call x1, Pallas kernels, decode_part(): pl.pallas_call(functools.partial(decode_kernel, len(keyvals), held), out_...  3.68 us
    pallas_call x2, Pallas kernels, route(): pl.pallas_call(functools.partial(route_kernel, block, len(got)), out_shap...  3.44 us
  transfers between devices with their start and end apart: 19, of which 7 were waited for; matrix products, arithmetic and copies ran while one was open for 3% of the time, Pallas kernels for 34%

profile of v2, /device:TPU:1, one launch (start us, length us, event | category | flops | bytes accessed | tf_op | source)
XLA Modules:
  0.0 169.5 jit_solution(18356983955107449584)
XLA Ops:
  0.7 2.5 %fusion.2 = (bf16[2,1,256,768]{3,2,1,0:T(8,128)(2,1)}, bf16[2,1,256,768]{3,2,1,0:T(8,128)(2,1)S(1)}) fusion(bf16[2,2,256,768]{3,2,1,0:T(8,128)(2,1)} %bitcast.21), kind=kLoop, calls=%fused_computation.10 | loop fusion | bytes 3145728 | tf_op jit(solution)/shard_map/slice | solution.py:571
  4.1 4.4 %collective-permute-start.2 = (bf16[528,768]{1,0:T(8,128)(2,1)}, bf16[528,768]{1,0:T(8,128)(2,1)}, u32[]{:S(2)}, u32[]{:S(2)}) collective-permute-start(bf16[528,768]{1,0:T(8,128)(2,1)} %fusion.1.refs_0_), channel_id=1, source_target_pairs={{0,4},{1,5},{2,6},{3,7},{4,0},{5,1},{6,2},{7,3},{8,12},{9,13},{10,... | collective-permute-start | bytes 2433032 | tf_op jit(solution)/shard_map/ppermute | solution.py:524
  8.5 2.7 %collective-permute-start.1 = (bf16[528,768]{1,0:T(8,128)(2,1)}, bf16[528,768]{1,0:T(8,128)(2,1)}, u32[]{:S(2)}, u32[]{:S(2)}) collective-permute-start(bf16[528,768]{1,0:T(8,128)(2,1)} %fusion.1.refs_0_), channel_id=1, source_target_pairs={{0,3},{1,0},{2,1},{3,2},{4,7},{5,4},{6,5},{7,6},{8,11},{9,8},{10,9... | collective-permute-start | bytes 2433032 | tf_op jit(solution)/shard_map/ppermute | solution.py:524
  12.9 6.1 %all-to-all-start = ((bf16[16,128,256]{2,1,0:T(8,128)(2,1)}), bf16[16,128,256]{2,1,0:T(8,128)(2,1)S(1)}, u32[]{:S(2)}, u32[]{:S(2)}) async-start(bf16[16,128,256]{2,1,0:T(8,128)(2,1)} %bitcast.5), calls=%async_computation | async-start | bytes 2097152 | tf_op jit(solution)/shard_map/all_to_all | solution.py:552
  19.9 3.0 %collective-permute-start.4 = (bf16[512,768]{1,0:T(8,128)(2,1)}, bf16[512,768]{1,0:T(8,128)(2,1)}, u32[]{:S(2)}, u32[]{:S(2)}) collective-permute-start(bf16[512,768]{1,0:T(8,128)(2,1)} %bitcast.2.refs_0_), channel_id=1, source_target_pairs={{0,3},{1,0},{2,1},{3,2},{4,7},{5,4},{6,5},{7,6},{8,11},{9,8},{10,9... | collective-permute-start | bytes 2359304 | tf_op jit(solution)/shard_map/ppermute | solution.py:524
  22.8 9.6 %collective-permute-done.2.refs_1_ = bf16[528,768]{1,0:T(8,128)(2,1)} collective-permute-done((bf16[528,768]{1,0:T(8,128)(2,1)}, bf16[528,768]{1,0:T(8,128)(2,1)}, u32[]{:S(2)}, u32[]{:S(2)}) %collective-permute-start.2) | collective-permute-done | bytes 811040 | tf_op jit(solution)/shard_map/ppermute | solution.py:524
  32.4 3.9 %collective-permute-start.3 = (bf16[512,768]{1,0:T(8,128)(2,1)}, bf16[512,768]{1,0:T(8,128)(2,1)}, u32[]{:S(2)}, u32[]{:S(2)}) collective-permute-start(bf16[512,768]{1,0:T(8,128)(2,1)} %bitcast.2.refs_0_), channel_id=1, source_target_pairs={{0,1},{1,2},{2,3},{3,0},{4,5},{5,6},{6,7},{7,4},{8,9},{9,10},{10,1... | collective-permute-start | bytes 2359304 | tf_op jit(solution)/shard_map/ppermute | solution.py:524
  37.7 7.7 %project.5.refs_6_ = f32[528,1024]{1,0:T(8,128)} custom-call(s32[4]{0:T(128)} %pad_add_fusion.ids, s32[2]{0:T(128)} %dynamic_slice.13.lives.live_ref, bf16[528,768]{1,0:T(8,128)(2,1)} %fusion.1.refs_0_, bf16[528,768]{1,0:T(8,128)(2,1)} %collective-permute-done.2.refs_1_, bf16[528,768]{1,0:T(8,128)(2,1)} %collective-permute-done.refs_2_, ...), custom_call_target="tpu_custom_call" | custom-call | flops 3321888768 | bytes 11698176 | tf_op jit(solution)/shard_map/project/pallas_call | solution.py:169
  47.1 7.6 %collective-permute-done.5.refs_1_ = bf16[512,768]{1,0:T(8,128)(2,1)} collective-permute-done((bf16[512,768]{1,0:T(8,128)(2,1)}, bf16[512,768]{1,0:T(8,128)(2,1)}, u32[]{:S(2)}, u32[]{:S(2)}) %collective-permute-start.5) | collective-permute-done | bytes 786464 | tf_op jit(solution)/shard_map/ppermute | solution.py:524
  57.5 7.0 %all-to-all-start.1 = ((bf16[16,128,256]{2,1,0:T(8,128)(2,1)}), bf16[16,128,256]{2,1,0:T(8,128)(2,1)S(1)}, u32[]{:S(2)}, u32[]{:S(2)}) async-start(bf16[16,128,256]{2,1,0:T(8,128)(2,1)} %route.2), calls=%async_computation.1 | async-start | bytes 2097152 | tf_op jit(solution)/shard_map/all_to_all | solution.py:552
  64.5 9.3 %collective-permute-done.7.refs_4_ = bf16[512,768]{1,0:T(8,128)(2,1)} collective-permute-done((bf16[512,768]{1,0:T(8,128)(2,1)}, bf16[512,768]{1,0:T(8,128)(2,1)}, u32[]{:S(2)}, u32[]{:S(2)}) %collective-permute-start.7) | collective-permute-done | bytes 786464 | tf_op jit(solution)/shard_map/ppermute | solution.py:524
  79.3 8.3 %project.6.refs_4_ = f32[512,1024]{1,0:T(8,128)} custom-call(s32[5]{0:T(128)} %stack.39.ids, s32[2]{0:T(128)} %dynamic_slice.13.lives.live_ref, bf16[512,768]{1,0:T(8,128)(2,1)} %bitcast.2.refs_0_, bf16[512,768]{1,0:T(8,128)(2,1)} %collective-permute-done.5.refs_1_, bf16[512,768]{1,0:T(8,128)(2,1)} %collective-permute-done.3.refs_2_, ...), custom_call_target="tpu_custom_call" | custom-call | flops 4026531840 | bytes 13893632 | tf_op jit(solution)/shard_map/project/pallas_call | solution.py:169
  87.6 4.8 %collective-permute-done.9.refs_2_ = bf16[528,768]{1,0:T(8,128)(2,1)} collective-permute-done((bf16[528,768]{1,0:T(8,128)(2,1)}, bf16[528,768]{1,0:T(8,128)(2,1)}, u32[]{:S(2)}, u32[]{:S(2)}) %collective-permute-start.9) | collective-permute-done | bytes 811040 | tf_op jit(solution)/shard_map/ppermute | solution.py:524
  92.5 2.7 %collective-permute-done.8.refs_1_ = bf16[528,768]{1,0:T(8,128)(2,1)} collective-permute-done((bf16[528,768]{1,0:T(8,128)(2,1)}, bf16[528,768]{1,0:T(8,128)(2,1)}, u32[]{:S(2)}, u32[]{:S(2)}) %collective-permute-start.8) | collective-permute-done | bytes 811040 | tf_op jit(solution)/shard_map/ppermute | solution.py:524
  95.2 4.3 %collective-permute-done.10.refs_3_ = bf16[528,768]{1,0:T(8,128)(2,1)} collective-permute-done((bf16[528,768]{1,0:T(8,128)(2,1)}, bf16[528,768]{1,0:T(8,128)(2,1)}, u32[]{:S(2)}, u32[]{:S(2)}) %collective-permute-start.10) | collective-permute-done | bytes 811040 | tf_op jit(solution)/shard_map/ppermute | solution.py:524
  101.5 8.4 %project.7 = (bf16[528,768]{1,0:T(8,128)(2,1)}, bf16[528,256]{1,0:T(8,128)(2,1)}, bf16[16,48,256]{2,1,0:T(8,128)(2,1)}) custom-call(s32[4]{0:T(128)} %pad_add_fusion.1.ids, s32[2]{0:T(128)} %dynamic_slice.13.lives.live_ref, bf16[528,768]{1,0:T(8,128)(2,1)} %collective-permute-done.6.refs_0_, bf16[528,768]{1,0:T(8,128)(2,1)} %collective-permute-done.8.refs_1_, ...), custom_call_target="tpu_custom_call" | custom-call | flops 3321888768 | bytes 11698176 | tf_op jit(solution)/shard_map/project/pallas_call | solution.py:169
  109.9 8.1 %all-to-all-start.2 = ((bf16[16,48,256]{2,1,0:T(8,128)(2,1)}), bf16[16,48,256]{2,1,0:T(8,128)(2,1)S(1)}, u32[]{:S(2)}, u32[]{:S(2)}) async-start(bf16[16,48,256]{2,1,0:T(8,128)(2,1)} %get-tuple-element.54), calls=%async_computation.2 | async-start | bytes 786432 | tf_op jit(solution)/shard_map/all_to_all | solution.py:552
  118.6 10.1 %prefill.2.refs_2_ = bf16[1024,768]{1,0:T(8,128)(2,1)} custom-call(s32[2]{0:T(128)} %copy-done.5, s32[2]{0:T(128)} %dynamic_slice.13.lives.live_ref, bf16[528,768]{1,0:T(8,128)(2,1)} %get-tuple-element.55.q_ref, bf16[2,1024,256]{2,1,0:T(8,128)(2,1)} %prefix_ref.5, bf16[528,256]{1,0:T(8,128)(2,1)} %get-tuple-element.58.refs_0_), custom_call_target="tpu_custom_call" | custom-call | flops 2013265920 | bytes 2621440 | tf_op jit(solution)/shard_map/prefill/pallas_call | solution.py:403
  128.7 4.1 %project.8 = (bf16[512,256]{1,0:T(8,128)(2,1)}, bf16[16,32,256]{2,1,0:T(8,128)(2,1)}) custom-call(s32[3]{0:T(128)} %pad_add_fusion.2.ids, s32[2]{0:T(128)} %dynamic_slice.13.lives.live_ref, bf16[512,768]{1,0:T(8,128)(2,1)} %collective-permute-done.11.refs_0_, bf16[512,768]{1,0:T(8,128)(2,1)} %collective-permute-done.12.refs_1_, ...), custom_call_target="tpu_custom_call" | custom-call | flops 603979776 | bytes 4063232 | tf_op jit(solution)/shard_map/project/pallas_call | solution.py:169
  132.8 5.2 %all-to-all-start.3 = ((bf16[16,32,256]{2,1,0:T(8,128)(2,1)}), bf16[16,32,256]{2,1,0:T(8,128)(2,1)S(1)}, u32[]{:S(2)}, u32[]{:S(2)}) async-start(bf16[16,32,256]{2,1,0:T(8,128)(2,1)} %get-tuple-element.66), calls=%async_computation.3 | async-start | bytes 524288 | tf_op jit(solution)/shard_map/all_to_all | solution.py:552
  138.6 3.7 %decode.1.refs_2_ = bf16[16,256]{1,0:T(8,128)(2,1)} custom-call(s32[2]{0:T(128)} %dynamic_slice.14.owner_ref, s32[2]{0:T(128)} %copy-done.5, s32[2]{0:T(128)} %dynamic_slice.13.lives.live_ref, bf16[16,48,256]{2,1,0:T(8,128)(2,1)} %copy-done, bf16[2,1024,256]{2,1,0:T(8,128)(2,1)} %prefix_ref.5, bf16[528,256]{1,0:T(8,128)(2,1)} %get-tuple-element.58.refs_0_, ...), custom_call_target="tpu_custom_call" | custom-call | flops 18874368 | bytes 1572864 | tf_op jit(solution)/shard_map/decode/pallas_call | solution.py:481
  142.3 6.1 %project.9.q_ref = bf16[512,768]{1,0:T(8,128)(2,1)} custom-call(s32[3]{0:T(128)} %pad_add_fusion.2.ids, s32[2]{0:T(128)} %dynamic_slice.13.lives.live_ref, bf16[512,768]{1,0:T(8,128)(2,1)} %collective-permute-done.11.refs_0_, bf16[512,768]{1,0:T(8,128)(2,1)} %collective-permute-done.12.refs_1_, bf16[512,768]{1,0:T(8,128)(2,1)} %collective-permute-done.13.refs_2_, ...), custom_call_target="tpu_custom_call" | custom-call | flops 1811939328 | bytes 7471104 | tf_op jit(solution)/shard_map/project/pallas_call | solution.py:169
  150.1 5.7 %all-to-all-start.4 = ((bf16[16,80,256]{2,1,0:T(8,128)(2,1)}), bf16[16,80,256]{2,1,0:T(8,128)(2,1)S(1)}, u32[]{:S(2)}, u32[]{:S(2)}) async-start(bf16[16,80,256]{2,1,0:T(8,128)(2,1)} %route.3), calls=%async_computation.4 | async-start | bytes 1310720 | tf_op jit(solution)/shard_map/all_to_all | solution.py:552
  156.9 11.2 %prefill.3 = bf16[1024,768]{1,0:T(8,128)(2,1)} custom-call(s32[2]{0:T(128)} %copy-done.5, s32[2]{0:T(128)} %dynamic_slice.13.lives.live_ref, bf16[512,768]{1,0:T(8,128)(2,1)} %project.9.q_ref, bf16[2,1024,256]{2,1,0:T(8,128)(2,1)} %prefix_ref.5, bf16[528,256]{1,0:T(8,128)(2,1)} %get-tuple-element.58.refs_0_, ...), custom_call_target="tpu_custom_call", output_to_operand_aliasing={{}: (6, {})} | custom-call | flops 2013265920 | bytes 2621440 | tf_op jit(solution)/shard_map/prefill/pallas_call | solution.py:403
  (58 shorter events, 22.3 us)
Async XLA Ops:
  0.6 10.6 %copy-start.6 = (s32[32]{0:T(128)S(1)}, s32[32]{0:T(128)}, u32[]{:S(2)}) copy-start(s32[32]{0:T(128)} %param.14) | copy-start | bytes 388
  0.7 10.7 %copy-start.3 = (bf16[2,1024,256]{2,1,0:T(8,128)(2,1)S(1)}, bf16[2,1024,256]{2,1,0:T(8,128)(2,1)}, u32[]{:S(2)}) copy-start(bf16[2,1024,256]{2,1,0:T(8,128)(2,1)} %prefix_ref.5) | copy-start | bytes 3145732
  4.1 28.4 %collective-permute-start.2 = (bf16[528,768]{1,0:T(8,128)(2,1)}, bf16[528,768]{1,0:T(8,128)(2,1)}, u32[]{:S(2)}, u32[]{:S(2)}) collective-permute-start(bf16[528,768]{1,0:T(8,128)(2,1)} %fusion.1.refs_0_), channel_id=1, source_target_pairs={{0,4},{1,5},{2,6},{3,7},{4,0},{5,1},{6,2},{7,3},{8,12},{9,13},{10,... | collective-permute-start | bytes 2433032 | tf_op jit(solution)/shard_map/ppermute | solution.py:524
  8.5 29.2 %collective-permute-start.1 = (bf16[528,768]{1,0:T(8,128)(2,1)}, bf16[528,768]{1,0:T(8,128)(2,1)}, u32[]{:S(2)}, u32[]{:S(2)}) collective-permute-start(bf16[528,768]{1,0:T(8,128)(2,1)} %fusion.1.refs_0_), channel_id=1, source_target_pairs={{0,3},{1,0},{2,1},{3,2},{4,7},{5,4},{6,5},{7,6},{8,11},{9,8},{10,9... | collective-permute-start | bytes 2433032 | tf_op jit(solution)/shard_map/ppermute | solution.py:524
  11.2 26.4 %collective-permute-start = (bf16[528,768]{1,0:T(8,128)(2,1)}, bf16[528,768]{1,0:T(8,128)(2,1)}, u32[]{:S(2)}, u32[]{:S(2)}) collective-permute-start(bf16[528,768]{1,0:T(8,128)(2,1)} %fusion.1.refs_0_), channel_id=1, source_target_pairs={{0,1},{1,2},{2,3},{3,0},{4,5},{5,6},{6,7},{7,4},{8,9},{9,10},{10,1... | collective-permute-start | bytes 2433032 | tf_op jit(solution)/shard_map/ppermute | solution.py:524
  12.9 23.4 %copy-start.7 = (s32[32]{0:T(128)S(1)}, s32[32]{0:T(128)}, u32[]{:S(2)}) copy-start(s32[32]{0:T(128)} %param.13) | copy-start | bytes 388
  12.9 24.7 %copy-start.8 = (s32[32]{0:T(128)S(1)}, s32[32]{0:T(128)}, u32[]{:S(2)}) copy-start(s32[32]{0:T(128)} %param.15) | copy-start | bytes 388
  12.9 32.5 %all-to-all-start = ((bf16[16,128,256]{2,1,0:T(8,128)(2,1)}), bf16[16,128,256]{2,1,0:T(8,128)(2,1)S(1)}, u32[]{:S(2)}, u32[]{:S(2)}) async-start(bf16[16,128,256]{2,1,0:T(8,128)(2,1)} %bitcast.5), calls=%async_computation | async-start | bytes 2097152 | tf_op jit(solution)/shard_map/all_to_all | solution.py:552
  19.0 35.7 %collective-permute-start.5 = (bf16[512,768]{1,0:T(8,128)(2,1)}, bf16[512,768]{1,0:T(8,128)(2,1)}, u32[]{:S(2)}, u32[]{:S(2)}) collective-permute-start(bf16[512,768]{1,0:T(8,128)(2,1)} %bitcast.2.refs_0_), channel_id=1, source_target_pairs={{0,4},{1,5},{2,6},{3,7},{4,0},{5,1},{6,2},{7,3},{8,12},{9,13},{10,... | collective-permute-start | bytes 2359304 | tf_op jit(solution)/shard_map/ppermute | solution.py:524
  19.9 34.8 %collective-permute-start.4 = (bf16[512,768]{1,0:T(8,128)(2,1)}, bf16[512,768]{1,0:T(8,128)(2,1)}, u32[]{:S(2)}, u32[]{:S(2)}) collective-permute-start(bf16[512,768]{1,0:T(8,128)(2,1)} %bitcast.2.refs_0_), channel_id=1, source_target_pairs={{0,3},{1,0},{2,1},{3,2},{4,7},{5,4},{6,5},{7,6},{8,11},{9,8},{10,9... | collective-permute-start | bytes 2359304 | tf_op jit(solution)/shard_map/ppermute | solution.py:524
  32.4 22.3 %collective-permute-start.3 = (bf16[512,768]{1,0:T(8,128)(2,1)}, bf16[512,768]{1,0:T(8,128)(2,1)}, u32[]{:S(2)}, u32[]{:S(2)}) collective-permute-start(bf16[512,768]{1,0:T(8,128)(2,1)} %bitcast.2.refs_0_), channel_id=1, source_target_pairs={{0,1},{1,2},{2,3},{3,0},{4,5},{5,6},{6,7},{7,4},{8,9},{9,10},{10,1... | collective-permute-start | bytes 2359304 | tf_op jit(solution)/shard_map/ppermute | solution.py:524
  54.7 20.0 %collective-permute-start.6 = (bf16[528,768]{1,0:T(8,128)(2,1)}, bf16[528,768]{1,0:T(8,128)(2,1)}, u32[]{:S(2)}, u32[]{:S(2)}) collective-permute-start(bf16[528,768]{1,0:T(8,128)(2,1)} %collective-permute-done.refs_2_), channel_id=1, source_target_pairs={{0,1},{1,2},{2,3},{3,0},{4,5},{5,6},{6,7},{7,4},{8,9},{9,10},{10,1... | collective-permute-start | bytes 2433032 | tf_op jit(solution)/shard_map/ppermute | solution.py:524
  56.0 17.8 %collective-permute-start.7 = (bf16[512,768]{1,0:T(8,128)(2,1)}, bf16[512,768]{1,0:T(8,128)(2,1)}, u32[]{:S(2)}, u32[]{:S(2)}) collective-permute-start(bf16[512,768]{1,0:T(8,128)(2,1)} %collective-permute-done.4.refs_3_), channel_id=1, source_target_pairs={{0,3},{1,0},{2,1},{3,2},{4,7},{5,4},{6,5},{7,6},{8,11},{9,8},{10,9... | collective-permute-start | bytes 2359304 | tf_op jit(solution)/shard_map/ppermute | solution.py:524
  57.5 30.1 %all-to-all-start.1 = ((bf16[16,128,256]{2,1,0:T(8,128)(2,1)}), bf16[16,128,256]{2,1,0:T(8,128)(2,1)S(1)}, u32[]{:S(2)}, u32[]{:S(2)}) async-start(bf16[16,128,256]{2,1,0:T(8,128)(2,1)} %route.2), calls=%async_computation.1 | async-start | bytes 2097152 | tf_op jit(solution)/shard_map/all_to_all | solution.py:552
  74.7 17.8 %collective-permute-start.9 = (bf16[528,768]{1,0:T(8,128)(2,1)}, bf16[528,768]{1,0:T(8,128)(2,1)}, u32[]{:S(2)}, u32[]{:S(2)}) collective-permute-start(bf16[528,768]{1,0:T(8,128)(2,1)} %collective-permute-done.2.refs_1_), channel_id=1, source_target_pairs={{0,3},{1,0},{2,1},{3,2},{4,7},{5,4},{6,5},{7,6},{8,11},{9,8},{10,9... | collective-permute-start | bytes 2433032 | tf_op jit(solution)/shard_map/ppermute | solution.py:524
  76.7 18.5 %collective-permute-start.8 = (bf16[528,768]{1,0:T(8,128)(2,1)}, bf16[528,768]{1,0:T(8,128)(2,1)}, u32[]{:S(2)}, u32[]{:S(2)}) collective-permute-start(bf16[528,768]{1,0:T(8,128)(2,1)} %collective-permute-done.2.refs_1_), channel_id=1, source_target_pairs={{0,1},{1,2},{2,3},{3,0},{4,5},{5,6},{6,7},{7,4},{8,9},{9,10},{10,1... | collective-permute-start | bytes 2433032 | tf_op jit(solution)/shard_map/ppermute | solution.py:524
  76.7 22.8 %collective-permute-start.10 = (bf16[528,768]{1,0:T(8,128)(2,1)}, bf16[528,768]{1,0:T(8,128)(2,1)}, u32[]{:S(2)}, u32[]{:S(2)}) collective-permute-start(bf16[528,768]{1,0:T(8,128)(2,1)} %collective-permute-done.6.refs_0_), channel_id=1, source_target_pairs={{0,4},{1,5},{2,6},{3,7},{4,0},{5,1},{6,2},{7,3},{8,12},{9,13},{10,... | collective-permute-start | bytes 2433032 | tf_op jit(solution)/shard_map/ppermute | solution.py:524
  99.5 29.2 %collective-permute-start.12 = (bf16[512,768]{1,0:T(8,128)(2,1)}, bf16[512,768]{1,0:T(8,128)(2,1)}, u32[]{:S(2)}, u32[]{:S(2)}) collective-permute-start(bf16[512,768]{1,0:T(8,128)(2,1)} %collective-permute-done.5.refs_1_), channel_id=1, source_target_pairs={{0,3},{1,0},{2,1},{3,2},{4,7},{5,4},{6,5},{7,6},{8,11},{9,8},{10,9... | collective-permute-start | bytes 2359304 | tf_op jit(solution)/shard_map/ppermute | solution.py:524
  99.5 29.2 %collective-permute-start.11 = (bf16[512,768]{1,0:T(8,128)(2,1)}, bf16[512,768]{1,0:T(8,128)(2,1)}, u32[]{:S(2)}, u32[]{:S(2)}) collective-permute-start(bf16[512,768]{1,0:T(8,128)(2,1)} %collective-permute-done.5.refs_1_), channel_id=1, source_target_pairs={{0,1},{1,2},{2,3},{3,0},{4,5},{5,6},{6,7},{7,4},{8,9},{9,10},{10,1... | collective-permute-start | bytes 2359304 | tf_op jit(solution)/shard_map/ppermute | solution.py:524
  100.9 27.8 %collective-permute-start.13 = (bf16[512,768]{1,0:T(8,128)(2,1)}, bf16[512,768]{1,0:T(8,128)(2,1)}, u32[]{:S(2)}, u32[]{:S(2)}) collective-permute-start(bf16[512,768]{1,0:T(8,128)(2,1)} %collective-permute-done.7.refs_4_), channel_id=1, source_target_pairs={{0,4},{1,5},{2,6},{3,7},{4,0},{5,1},{6,2},{7,3},{8,12},{9,13},{10,... | collective-permute-start | bytes 2359304 | tf_op jit(solution)/shard_map/ppermute | solution.py:524
  109.9 18.8 %all-to-all-start.2 = ((bf16[16,48,256]{2,1,0:T(8,128)(2,1)}), bf16[16,48,256]{2,1,0:T(8,128)(2,1)S(1)}, u32[]{:S(2)}, u32[]{:S(2)}) async-start(bf16[16,48,256]{2,1,0:T(8,128)(2,1)} %get-tuple-element.54), calls=%async_computation.2 | async-start | bytes 786432 | tf_op jit(solution)/shard_map/all_to_all | solution.py:552
  132.8 15.6 %all-to-all-start.3 = ((bf16[16,32,256]{2,1,0:T(8,128)(2,1)}), bf16[16,32,256]{2,1,0:T(8,128)(2,1)S(1)}, u32[]{:S(2)}, u32[]{:S(2)}) async-start(bf16[16,32,256]{2,1,0:T(8,128)(2,1)} %get-tuple-element.66), calls=%async_computation.3 | async-start | bytes 524288 | tf_op jit(solution)/shard_map/all_to_all | solution.py:552
  142.3 6.2 %copy-start.2 = (bf16[16,256]{1,0:T(8,128)(2,1)S(1)}, bf16[16,256]{1,0:T(8,128)(2,1)}, u32[]{:S(2)}) copy-start(bf16[16,256]{1,0:T(8,128)(2,1)} %decode.1.refs_2_) | copy-start | bytes 24580
  150.1 18.0 %all-to-all-start.4 = ((bf16[16,80,256]{2,1,0:T(8,128)(2,1)}), bf16[16,80,256]{2,1,0:T(8,128)(2,1)S(1)}, u32[]{:S(2)}, u32[]{:S(2)}) async-start(bf16[16,80,256]{2,1,0:T(8,128)(2,1)} %route.3), calls=%async_computation.4 | async-start | bytes 1310720 | tf_op jit(solution)/shard_map/all_to_all | solution.py:552
  (4 other events, 14.4 us)

commit v3 on v2

--- a/solution.py
+++ b/solution.py
@@ -571,20 +571,21 @@
     second = by_req[:, 1].reshape(rows, depth)
 
     up0, down0, across0 = send(first, 0, 1), send(first, 0, -1), send(first, 1, 0)
-    up1, down1, across1 = send(second, 0, 1), send(second, 0, -1), send(second, 1, 0)
+    up1, down1 = send(second, 0, 1), send(second, 0, -1)
     prefix_got = exchange(for_spread(zero_dead(prefix_cache, 0, fills)))
     prefix_sent = route([prefix_got], source, ctx_len // replicas)
     early0 = project(
         [[first], [across0], [up0], [down0]], ids[:4], both, lives, out_type=jnp.float32
     )[0]
-    up0, down0, across0, up1, down1, across1, prefix_sent, early0 = phase_end(
-        up0, down0, across0, up1, down1, across1, prefix_sent, early0
+    up0, down0, across0, up1, down1, second, prefix_sent, early0 = phase_end(
+        up0, down0, across0, up1, down1, second, prefix_sent, early0
     )
 
     far0 = send(up0, 0, 1)
     far1 = send(down1, 0, -1)
+    across1 = send(second, 1, 0)
     prefix_home = exchange(prefix_sent)
-    far0, far1, across0, across1, early0 = phase_end(far0, far1, across0, across1, early0)
+    far0, far1, across0, early0 = phase_end(far0, far1, across0, early0)
 
     across_up0, across_down0 = send(across0, 0, 1), send(across0, 0, -1)
     across_far0 = send(far0, 1, 0)

time: 170 us -> 169 us (level)
  waiting for transfers between devices: 39.2 us -> 42.6 us
  Pallas kernels: 65.4 us -> 62.3 us
  starting transfers between devices: 55.4 us -> 52.3 us
    ppermute x14, starting transfers between devices: 23.2 us -> 17.6 us  [send(): return lax.ppermute(x, 'tensor', moved(plane, shift))]
    pallas_call x2, Pallas kernels: 21.3 us -> 18.2 us  [prefill_part(): pl.pallas_call(functools.partial(prefill_kernel, part, ctx_len), out_shap...]
    all_to_all x5, starting transfers between devices: 32.2 us -> 34.7 us  [exchange(): return lax.all_to_all(x, 'replica', split_axis=0, concat_axis=0, tiled=True)]
    ppermute x14, waiting for transfers between devices: 39.2 us -> 41 us  [send(): return lax.ppermute(x, 'tensor', moved(plane, shift))]
  transfers between devices with their start and end apart: 19 -> 19, of which waited for: 7 -> 10; matrix products, arithmetic and copies ran while one was open for 3% -> 3% of each run, Pallas kernels for 34% -> 33%
where the time goes in v3:
time: 169 us; the launch traced here: 167 us
  Pallas kernels  62.3 us (37%)
  starting transfers between devices  52.3 us (31%)
  waiting for transfers between devices  42.6 us (25%)
  local copies, waits for them, and re-layouts  5.48 us (3%)
  other arithmetic  3.34 us (2%)
    ppermute x14, waiting for transfers between devices, send(): return lax.ppermute(x, 'tensor', moved(plane, shift))  41 us
    all_to_all x5, starting transfers between devices, exchange(): return lax.all_to_all(x, 'replica', split_axis=0, concat_axis=0, tiled=True)  34.7 us
    pallas_call x5, Pallas kernels, project(): pl.pallas_call(functools.partial(project_kernel, (groups, counts, depth),...  34.6 us
    pallas_call x2, Pallas kernels, prefill_part(): pl.pallas_call(functools.partial(prefill_kernel, part, ctx_len), out_shap...  18.2 us
    ppermute x14, starting transfers between devices, send(): return lax.ppermute(x, 'tensor', moved(plane, shift))  17.6 us
    pallas_call x1, Pallas kernels, decode_part(): pl.pallas_call(functools.partial(decode_kernel, len(keyvals), held), out_...  3.68 us
    pallas_call x2, Pallas kernels, route(): pl.pallas_call(functools.partial(route_kernel, block, len(got)), out_shap...  3.44 us
  transfers between devices with their start and end apart: 19, of which 10 were waited for; matrix products, arithmetic and copies ran while one was open for 3% of the time, Pallas kernels for 33%

profile of v3, /device:TPU:1, one launch (start us, length us, event | category | flops | bytes accessed | tf_op | source)
XLA Modules:
  0.0 166.9 jit_solution(14672696287689351670)
XLA Ops:
  0.7 2.5 %fusion.2 = (bf16[2,1,256,768]{3,2,1,0:T(8,128)(2,1)}, bf16[2,1,256,768]{3,2,1,0:T(8,128)(2,1)S(1)}) fusion(bf16[2,2,256,768]{3,2,1,0:T(8,128)(2,1)} %bitcast.21), kind=kLoop, calls=%fused_computation.10 | loop fusion | bytes 3145728 | tf_op jit(solution)/shard_map/slice | solution.py:571
  4.1 4.4 %collective-permute-start.2 = (bf16[528,768]{1,0:T(8,128)(2,1)}, bf16[528,768]{1,0:T(8,128)(2,1)}, u32[]{:S(2)}, u32[]{:S(2)}) collective-permute-start(bf16[528,768]{1,0:T(8,128)(2,1)} %fusion.1.refs_0_), channel_id=1, source_target_pairs={{0,4},{1,5},{2,6},{3,7},{4,0},{5,1},{6,2},{7,3},{8,12},{9,13},{10,... | collective-permute-start | bytes 2433032 | tf_op jit(solution)/shard_map/ppermute | solution.py:524
  8.5 2.7 %collective-permute-start.1 = (bf16[528,768]{1,0:T(8,128)(2,1)}, bf16[528,768]{1,0:T(8,128)(2,1)}, u32[]{:S(2)}, u32[]{:S(2)}) collective-permute-start(bf16[528,768]{1,0:T(8,128)(2,1)} %fusion.1.refs_0_), channel_id=1, source_target_pairs={{0,3},{1,0},{2,1},{3,2},{4,7},{5,4},{6,5},{7,6},{8,11},{9,8},{10,9... | collective-permute-start | bytes 2433032 | tf_op jit(solution)/shard_map/ppermute | solution.py:524
  12.9 6.1 %all-to-all-start = ((bf16[16,128,256]{2,1,0:T(8,128)(2,1)}), bf16[16,128,256]{2,1,0:T(8,128)(2,1)S(1)}, u32[]{:S(2)}, u32[]{:S(2)}) async-start(bf16[16,128,256]{2,1,0:T(8,128)(2,1)} %bitcast.5), calls=%async_computation | async-start | bytes 2097152 | tf_op jit(solution)/shard_map/all_to_all | solution.py:552
  19.0 3.0 %collective-permute-start.4 = (bf16[512,768]{1,0:T(8,128)(2,1)}, bf16[512,768]{1,0:T(8,128)(2,1)}, u32[]{:S(2)}, u32[]{:S(2)}) collective-permute-start(bf16[512,768]{1,0:T(8,128)(2,1)} %bitcast.2.refs_0_), channel_id=1, source_target_pairs={{0,3},{1,0},{2,1},{3,2},{4,7},{5,4},{6,5},{7,6},{8,11},{9,8},{10,9... | collective-permute-start | bytes 2359304 | tf_op jit(solution)/shard_map/ppermute | solution.py:524
  23.3 9.1 %collective-permute-done.2.refs_1_ = bf16[528,768]{1,0:T(8,128)(2,1)} collective-permute-done((bf16[528,768]{1,0:T(8,128)(2,1)}, bf16[528,768]{1,0:T(8,128)(2,1)}, u32[]{:S(2)}, u32[]{:S(2)}) %collective-permute-start.2) | collective-permute-done | bytes 811040 | tf_op jit(solution)/shard_map/ppermute | solution.py:524
  32.4 7.7 %project.5.refs_6_ = f32[528,1024]{1,0:T(8,128)} custom-call(s32[4]{0:T(128)} %pad_add_fusion.ids, s32[2]{0:T(128)} %dynamic_slice.13.lives.live_ref, bf16[528,768]{1,0:T(8,128)(2,1)} %fusion.1.refs_0_, bf16[528,768]{1,0:T(8,128)(2,1)} %collective-permute-done.2.refs_1_, bf16[528,768]{1,0:T(8,128)(2,1)} %collective-permute-done.refs_2_, ...), custom_call_target="tpu_custom_call" | custom-call | flops 3321888768 | bytes 11698176 | tf_op jit(solution)/shard_map/project/pallas_call | solution.py:169
  41.9 2.9 %collective-permute-done.4.refs_3_ = bf16[512,768]{1,0:T(8,128)(2,1)} collective-permute-done((bf16[512,768]{1,0:T(8,128)(2,1)}, bf16[512,768]{1,0:T(8,128)(2,1)}, u32[]{:S(2)}, u32[]{:S(2)}) %collective-permute-start.4) | collective-permute-done | bytes 786464 | tf_op jit(solution)/shard_map/ppermute | solution.py:524
  44.8 3.1 %collective-permute-done.3.refs_2_ = bf16[512,768]{1,0:T(8,128)(2,1)} collective-permute-done((bf16[512,768]{1,0:T(8,128)(2,1)}, bf16[512,768]{1,0:T(8,128)(2,1)}, u32[]{:S(2)}, u32[]{:S(2)}) %collective-permute-start.3) | collective-permute-done | bytes 786464 | tf_op jit(solution)/shard_map/ppermute | solution.py:524
  47.9 2.7 %collective-permute-start.6 = (bf16[512,768]{1,0:T(8,128)(2,1)}, bf16[512,768]{1,0:T(8,128)(2,1)}, u32[]{:S(2)}, u32[]{:S(2)}) collective-permute-start(bf16[512,768]{1,0:T(8,128)(2,1)} %collective-permute-done.4.refs_3_), channel_id=1, source_target_pairs={{0,3},{1,0},{2,1},{3,2},{4,7},{5,4},{6,5},{7,6},{8,11},{9,8},{10,9... | collective-permute-start | bytes 2359304 | tf_op jit(solution)/shard_map/ppermute | solution.py:524
  50.9 7.7 %all-to-all-start.1 = ((bf16[16,128,256]{2,1,0:T(8,128)(2,1)}), bf16[16,128,256]{2,1,0:T(8,128)(2,1)S(1)}, u32[]{:S(2)}, u32[]{:S(2)}) async-start(bf16[16,128,256]{2,1,0:T(8,128)(2,1)} %route.2), calls=%async_computation.1 | async-start | bytes 2097152 | tf_op jit(solution)/shard_map/all_to_all | solution.py:552
  58.6 6.7 %collective-permute-done.6.refs_4_ = bf16[512,768]{1,0:T(8,128)(2,1)} collective-permute-done((bf16[512,768]{1,0:T(8,128)(2,1)}, bf16[512,768]{1,0:T(8,128)(2,1)}, u32[]{:S(2)}, u32[]{:S(2)}) %collective-permute-start.6) | collective-permute-done | bytes 786464 | tf_op jit(solution)/shard_map/ppermute | solution.py:524
  69.9 4.7 %collective-permute-done.10.refs_1_ = bf16[512,768]{1,0:T(8,128)(2,1)} collective-permute-done((bf16[512,768]{1,0:T(8,128)(2,1)}, bf16[512,768]{1,0:T(8,128)(2,1)}, u32[]{:S(2)}, u32[]{:S(2)}) %collective-permute-start.10) | collective-permute-done | bytes 786464 | tf_op jit(solution)/shard_map/ppermute | solution.py:524
  74.7 8.3 %project.6.refs_4_ = f32[512,1024]{1,0:T(8,128)} custom-call(s32[5]{0:T(128)} %stack.39.ids, s32[2]{0:T(128)} %dynamic_slice.13.lives.live_ref, bf16[512,768]{1,0:T(8,128)(2,1)} %bitcast.2.refs_0_, bf16[512,768]{1,0:T(8,128)(2,1)} %collective-permute-done.10.refs_1_, bf16[512,768]{1,0:T(8,128)(2,1)} %collective-permute-done.3.refs_2_, ...), custom_call_target="tpu_custom_call" | custom-call | flops 4026531840 | bytes 13893632 | tf_op jit(solution)/shard_map/project/pallas_call | solution.py:169
  86.2 11.2 %collective-permute-done.9.refs_3_ = bf16[528,768]{1,0:T(8,128)(2,1)} collective-permute-done((bf16[528,768]{1,0:T(8,128)(2,1)}, bf16[528,768]{1,0:T(8,128)(2,1)}, u32[]{:S(2)}, u32[]{:S(2)}) %collective-permute-start.9) | collective-permute-done | bytes 811040 | tf_op jit(solution)/shard_map/ppermute | solution.py:524
  100.0 8.4 %project.7 = (bf16[528,768]{1,0:T(8,128)(2,1)}, bf16[528,256]{1,0:T(8,128)(2,1)}, bf16[16,48,256]{2,1,0:T(8,128)(2,1)}) custom-call(s32[4]{0:T(128)} %pad_add_fusion.1.ids, s32[2]{0:T(128)} %dynamic_slice.13.lives.live_ref, bf16[528,768]{1,0:T(8,128)(2,1)} %collective-permute-done.5.refs_0_, bf16[528,768]{1,0:T(8,128)(2,1)} %collective-permute-done.7.refs_1_, ...), custom_call_target="tpu_custom_call" | custom-call | flops 3321888768 | bytes 11698176 | tf_op jit(solution)/shard_map/project/pallas_call | solution.py:169
  108.4 8.9 %all-to-all-start.2 = ((bf16[16,48,256]{2,1,0:T(8,128)(2,1)}), bf16[16,48,256]{2,1,0:T(8,128)(2,1)S(1)}, u32[]{:S(2)}, u32[]{:S(2)}) async-start(bf16[16,48,256]{2,1,0:T(8,128)(2,1)} %get-tuple-element.52), calls=%async_computation.2 | async-start | bytes 786432 | tf_op jit(solution)/shard_map/all_to_all | solution.py:552
  117.9 8.6 %prefill.2.refs_2_ = bf16[1024,768]{1,0:T(8,128)(2,1)} custom-call(s32[2]{0:T(128)} %copy-done.5, s32[2]{0:T(128)} %dynamic_slice.13.lives.live_ref, bf16[528,768]{1,0:T(8,128)(2,1)} %get-tuple-element.53.q_ref, bf16[2,1024,256]{2,1,0:T(8,128)(2,1)} %prefix_ref.5, bf16[528,256]{1,0:T(8,128)(2,1)} %get-tuple-element.56.refs_0_), custom_call_target="tpu_custom_call" | custom-call | flops 2013265920 | bytes 2621440 | tf_op jit(solution)/shard_map/prefill/pallas_call | solution.py:403
  126.6 4.1 %project.8 = (bf16[512,256]{1,0:T(8,128)(2,1)}, bf16[16,32,256]{2,1,0:T(8,128)(2,1)}) custom-call(s32[3]{0:T(128)} %pad_add_fusion.2.ids, s32[2]{0:T(128)} %dynamic_slice.13.lives.live_ref, bf16[512,768]{1,0:T(8,128)(2,1)} %collective-permute-done.11.refs_0_, bf16[512,768]{1,0:T(8,128)(2,1)} %collective-permute-done.12.refs_1_, ...), custom_call_target="tpu_custom_call" | custom-call | flops 603979776 | bytes 4063232 | tf_op jit(solution)/shard_map/project/pallas_call | solution.py:169
  130.6 6.2 %all-to-all-start.3 = ((bf16[16,32,256]{2,1,0:T(8,128)(2,1)}), bf16[16,32,256]{2,1,0:T(8,128)(2,1)S(1)}, u32[]{:S(2)}, u32[]{:S(2)}) async-start(bf16[16,32,256]{2,1,0:T(8,128)(2,1)} %get-tuple-element.64), calls=%async_computation.3 | async-start | bytes 524288 | tf_op jit(solution)/shard_map/all_to_all | solution.py:552
  137.4 3.7 %decode.1.refs_2_ = bf16[16,256]{1,0:T(8,128)(2,1)} custom-call(s32[2]{0:T(128)} %dynamic_slice.14.owner_ref, s32[2]{0:T(128)} %copy-done.5, s32[2]{0:T(128)} %dynamic_slice.13.lives.live_ref, bf16[16,48,256]{2,1,0:T(8,128)(2,1)} %copy-done, bf16[2,1024,256]{2,1,0:T(8,128)(2,1)} %prefix_ref.5, bf16[528,256]{1,0:T(8,128)(2,1)} %get-tuple-element.56.refs_0_, ...), custom_call_target="tpu_custom_call" | custom-call | flops 18874368 | bytes 1572864 | tf_op jit(solution)/shard_map/decode/pallas_call | solution.py:481
  141.1 6.1 %project.9.q_ref = bf16[512,768]{1,0:T(8,128)(2,1)} custom-call(s32[3]{0:T(128)} %pad_add_fusion.2.ids, s32[2]{0:T(128)} %dynamic_slice.13.lives.live_ref, bf16[512,768]{1,0:T(8,128)(2,1)} %collective-permute-done.11.refs_0_, bf16[512,768]{1,0:T(8,128)(2,1)} %collective-permute-done.12.refs_1_, bf16[512,768]{1,0:T(8,128)(2,1)} %collective-permute-done.13.refs_2_, ...), custom_call_target="tpu_custom_call" | custom-call | flops 1811939328 | bytes 7471104 | tf_op jit(solution)/shard_map/project/pallas_call | solution.py:169
  148.9 5.7 %all-to-all-start.4 = ((bf16[16,80,256]{2,1,0:T(8,128)(2,1)}), bf16[16,80,256]{2,1,0:T(8,128)(2,1)S(1)}, u32[]{:S(2)}, u32[]{:S(2)}) async-start(bf16[16,80,256]{2,1,0:T(8,128)(2,1)} %route.3), calls=%async_computation.4 | async-start | bytes 1310720 | tf_op jit(solution)/shard_map/all_to_all | solution.py:552
  155.7 9.6 %prefill.3 = bf16[1024,768]{1,0:T(8,128)(2,1)} custom-call(s32[2]{0:T(128)} %copy-done.5, s32[2]{0:T(128)} %dynamic_slice.13.lives.live_ref, bf16[512,768]{1,0:T(8,128)(2,1)} %project.9.q_ref, bf16[2,1024,256]{2,1,0:T(8,128)(2,1)} %prefix_ref.5, bf16[528,256]{1,0:T(8,128)(2,1)} %get-tuple-element.56.refs_0_, ...), custom_call_target="tpu_custom_call", output_to_operand_aliasing={{}: (6, {})} | custom-call | flops 2013265920 | bytes 2621440 | tf_op jit(solution)/shard_map/prefill/pallas_call | solution.py:403
  (58 shorter events, 21.9 us)
Async XLA Ops:
  0.6 10.6 %copy-start.6 = (s32[32]{0:T(128)S(1)}, s32[32]{0:T(128)}, u32[]{:S(2)}) copy-start(s32[32]{0:T(128)} %param.14) | copy-start | bytes 388
  0.7 10.7 %copy-start.3 = (bf16[2,1024,256]{2,1,0:T(8,128)(2,1)S(1)}, bf16[2,1024,256]{2,1,0:T(8,128)(2,1)}, u32[]{:S(2)}) copy-start(bf16[2,1024,256]{2,1,0:T(8,128)(2,1)} %prefix_ref.5) | copy-start | bytes 3145732
  4.1 28.4 %collective-permute-start.2 = (bf16[528,768]{1,0:T(8,128)(2,1)}, bf16[528,768]{1,0:T(8,128)(2,1)}, u32[]{:S(2)}, u32[]{:S(2)}) collective-permute-start(bf16[528,768]{1,0:T(8,128)(2,1)} %fusion.1.refs_0_), channel_id=1, source_target_pairs={{0,4},{1,5},{2,6},{3,7},{4,0},{5,1},{6,2},{7,3},{8,12},{9,13},{10,... | collective-permute-start | bytes 2433032 | tf_op jit(solution)/shard_map/ppermute | solution.py:524
  8.5 23.9 %collective-permute-start.1 = (bf16[528,768]{1,0:T(8,128)(2,1)}, bf16[528,768]{1,0:T(8,128)(2,1)}, u32[]{:S(2)}, u32[]{:S(2)}) collective-permute-start(bf16[528,768]{1,0:T(8,128)(2,1)} %fusion.1.refs_0_), channel_id=1, source_target_pairs={{0,3},{1,0},{2,1},{3,2},{4,7},{5,4},{6,5},{7,6},{8,11},{9,8},{10,9... | collective-permute-start | bytes 2433032 | tf_op jit(solution)/shard_map/ppermute | solution.py:524
  11.2 21.2 %collective-permute-start = (bf16[528,768]{1,0:T(8,128)(2,1)}, bf16[528,768]{1,0:T(8,128)(2,1)}, u32[]{:S(2)}, u32[]{:S(2)}) collective-permute-start(bf16[528,768]{1,0:T(8,128)(2,1)} %fusion.1.refs_0_), channel_id=1, source_target_pairs={{0,1},{1,2},{2,3},{3,0},{4,5},{5,6},{6,7},{7,4},{8,9},{9,10},{10,1... | collective-permute-start | bytes 2433032 | tf_op jit(solution)/shard_map/ppermute | solution.py:524
  12.9 9.1 %copy-start.7 = (s32[32]{0:T(128)S(1)}, s32[32]{0:T(128)}, u32[]{:S(2)}) copy-start(s32[32]{0:T(128)} %param.13) | copy-start | bytes 388
  12.9 10.3 %copy-start.8 = (s32[32]{0:T(128)S(1)}, s32[32]{0:T(128)}, u32[]{:S(2)}) copy-start(s32[32]{0:T(128)} %param.15) | copy-start | bytes 388
  12.9 27.2 %all-to-all-start = ((bf16[16,128,256]{2,1,0:T(8,128)(2,1)}), bf16[16,128,256]{2,1,0:T(8,128)(2,1)S(1)}, u32[]{:S(2)}, u32[]{:S(2)}) async-start(bf16[16,128,256]{2,1,0:T(8,128)(2,1)} %bitcast.5), calls=%async_computation | async-start | bytes 2097152 | tf_op jit(solution)/shard_map/all_to_all | solution.py:552
  19.0 25.8 %collective-permute-start.4 = (bf16[512,768]{1,0:T(8,128)(2,1)}, bf16[512,768]{1,0:T(8,128)(2,1)}, u32[]{:S(2)}, u32[]{:S(2)}) collective-permute-start(bf16[512,768]{1,0:T(8,128)(2,1)} %bitcast.2.refs_0_), channel_id=1, source_target_pairs={{0,3},{1,0},{2,1},{3,2},{4,7},{5,4},{6,5},{7,6},{8,11},{9,8},{10,9... | collective-permute-start | bytes 2359304 | tf_op jit(solution)/shard_map/ppermute | solution.py:524
  22.0 26.0 %collective-permute-start.3 = (bf16[512,768]{1,0:T(8,128)(2,1)}, bf16[512,768]{1,0:T(8,128)(2,1)}, u32[]{:S(2)}, u32[]{:S(2)}) collective-permute-start(bf16[512,768]{1,0:T(8,128)(2,1)} %bitcast.2.refs_0_), channel_id=1, source_target_pairs={{0,1},{1,2},{2,3},{3,0},{4,5},{5,6},{6,7},{7,4},{8,9},{9,10},{10,1... | collective-permute-start | bytes 2359304 | tf_op jit(solution)/shard_map/ppermute | solution.py:524
  47.9 18.9 %collective-permute-start.5 = (bf16[528,768]{1,0:T(8,128)(2,1)}, bf16[528,768]{1,0:T(8,128)(2,1)}, u32[]{:S(2)}, u32[]{:S(2)}) collective-permute-start(bf16[528,768]{1,0:T(8,128)(2,1)} %collective-permute-done.refs_2_), channel_id=1, source_target_pairs={{0,1},{1,2},{2,3},{3,0},{4,5},{5,6},{6,7},{7,4},{8,9},{9,10},{10,1... | collective-permute-start | bytes 2433032 | tf_op jit(solution)/shard_map/ppermute | solution.py:524
  47.9 17.4 %collective-permute-start.6 = (bf16[512,768]{1,0:T(8,128)(2,1)}, bf16[512,768]{1,0:T(8,128)(2,1)}, u32[]{:S(2)}, u32[]{:S(2)}) collective-permute-start(bf16[512,768]{1,0:T(8,128)(2,1)} %collective-permute-done.4.refs_3_), channel_id=1, source_target_pairs={{0,3},{1,0},{2,1},{3,2},{4,7},{5,4},{6,5},{7,6},{8,11},{9,8},{10,9... | collective-permute-start | bytes 2359304 | tf_op jit(solution)/shard_map/ppermute | solution.py:524
  50.6 24.1 %collective-permute-start.10 = (bf16[512,768]{1,0:T(8,128)(2,1)}, bf16[512,768]{1,0:T(8,128)(2,1)}, u32[]{:S(2)}, u32[]{:S(2)}) collective-permute-start(bf16[512,768]{1,0:T(8,128)(2,1)} %bitcast.2.refs_0_), channel_id=1, source_target_pairs={{0,4},{1,5},{2,6},{3,7},{4,0},{5,1},{6,2},{7,3},{8,12},{9,13},{10,... | collective-permute-start | bytes 2359304 | tf_op jit(solution)/shard_map/ppermute | solution.py:524
  50.9 33.6 %all-to-all-start.1 = ((bf16[16,128,256]{2,1,0:T(8,128)(2,1)}), bf16[16,128,256]{2,1,0:T(8,128)(2,1)S(1)}, u32[]{:S(2)}, u32[]{:S(2)}) async-start(bf16[16,128,256]{2,1,0:T(8,128)(2,1)} %route.2), calls=%async_computation.1 | async-start | bytes 2097152 | tf_op jit(solution)/shard_map/all_to_all | solution.py:552
  66.9 17.7 %collective-permute-start.8 = (bf16[528,768]{1,0:T(8,128)(2,1)}, bf16[528,768]{1,0:T(8,128)(2,1)}, u32[]{:S(2)}, u32[]{:S(2)}) collective-permute-start(bf16[528,768]{1,0:T(8,128)(2,1)} %collective-permute-done.2.refs_1_), channel_id=1, source_target_pairs={{0,3},{1,0},{2,1},{3,2},{4,7},{5,4},{6,5},{7,6},{8,11},{9,8},{10,9... | collective-permute-start | bytes 2433032 | tf_op jit(solution)/shard_map/ppermute | solution.py:524
  68.7 17.4 %collective-permute-start.7 = (bf16[528,768]{1,0:T(8,128)(2,1)}, bf16[528,768]{1,0:T(8,128)(2,1)}, u32[]{:S(2)}, u32[]{:S(2)}) collective-permute-start(bf16[528,768]{1,0:T(8,128)(2,1)} %collective-permute-done.2.refs_1_), channel_id=1, source_target_pairs={{0,1},{1,2},{2,3},{3,0},{4,5},{5,6},{6,7},{7,4},{8,9},{9,10},{10,1... | collective-permute-start | bytes 2433032 | tf_op jit(solution)/shard_map/ppermute | solution.py:524
  68.7 28.6 %collective-permute-start.9 = (bf16[528,768]{1,0:T(8,128)(2,1)}, bf16[528,768]{1,0:T(8,128)(2,1)}, u32[]{:S(2)}, u32[]{:S(2)}) collective-permute-start(bf16[528,768]{1,0:T(8,128)(2,1)} %collective-permute-done.5.refs_0_), channel_id=1, source_target_pairs={{0,4},{1,5},{2,6},{3,7},{4,0},{5,1},{6,2},{7,3},{8,12},{9,13},{10,... | collective-permute-start | bytes 2433032 | tf_op jit(solution)/shard_map/ppermute | solution.py:524
  97.3 29.2 %collective-permute-start.12 = (bf16[512,768]{1,0:T(8,128)(2,1)}, bf16[512,768]{1,0:T(8,128)(2,1)}, u32[]{:S(2)}, u32[]{:S(2)}) collective-permute-start(bf16[512,768]{1,0:T(8,128)(2,1)} %collective-permute-done.10.refs_1_), channel_id=1, source_target_pairs={{0,3},{1,0},{2,1},{3,2},{4,7},{5,4},{6,5},{7,6},{8,11},{9,8},{10,9... | collective-permute-start | bytes 2359304 | tf_op jit(solution)/shard_map/ppermute | solution.py:524
  97.6 28.9 %collective-permute-start.11 = (bf16[512,768]{1,0:T(8,128)(2,1)}, bf16[512,768]{1,0:T(8,128)(2,1)}, u32[]{:S(2)}, u32[]{:S(2)}) collective-permute-start(bf16[512,768]{1,0:T(8,128)(2,1)} %collective-permute-done.10.refs_1_), channel_id=1, source_target_pairs={{0,1},{1,2},{2,3},{3,0},{4,5},{5,6},{6,7},{7,4},{8,9},{9,10},{10,1... | collective-permute-start | bytes 2359304 | tf_op jit(solution)/shard_map/ppermute | solution.py:524
  98.8 27.7 %collective-permute-start.13 = (bf16[512,768]{1,0:T(8,128)(2,1)}, bf16[512,768]{1,0:T(8,128)(2,1)}, u32[]{:S(2)}, u32[]{:S(2)}) collective-permute-start(bf16[512,768]{1,0:T(8,128)(2,1)} %collective-permute-done.6.refs_4_), channel_id=1, source_target_pairs={{0,4},{1,5},{2,6},{3,7},{4,0},{5,1},{6,2},{7,3},{8,12},{9,13},{10,... | collective-permute-start | bytes 2359304 | tf_op jit(solution)/shard_map/ppermute | solution.py:524
  108.4 18.1 %all-to-all-start.2 = ((bf16[16,48,256]{2,1,0:T(8,128)(2,1)}), bf16[16,48,256]{2,1,0:T(8,128)(2,1)S(1)}, u32[]{:S(2)}, u32[]{:S(2)}) async-start(bf16[16,48,256]{2,1,0:T(8,128)(2,1)} %get-tuple-element.52), calls=%async_computation.2 | async-start | bytes 786432 | tf_op jit(solution)/shard_map/all_to_all | solution.py:552
  130.6 16.6 %all-to-all-start.3 = ((bf16[16,32,256]{2,1,0:T(8,128)(2,1)}), bf16[16,32,256]{2,1,0:T(8,128)(2,1)S(1)}, u32[]{:S(2)}, u32[]{:S(2)}) async-start(bf16[16,32,256]{2,1,0:T(8,128)(2,1)} %get-tuple-element.64), calls=%async_computation.3 | async-start | bytes 524288 | tf_op jit(solution)/shard_map/all_to_all | solution.py:552
  141.1 6.2 %copy-start.2 = (bf16[16,256]{1,0:T(8,128)(2,1)S(1)}, bf16[16,256]{1,0:T(8,128)(2,1)}, u32[]{:S(2)}) copy-start(bf16[16,256]{1,0:T(8,128)(2,1)} %decode.1.refs_2_) | copy-start | bytes 24580
  148.9 16.5 %all-to-all-start.4 = ((bf16[16,80,256]{2,1,0:T(8,128)(2,1)}), bf16[16,80,256]{2,1,0:T(8,128)(2,1)S(1)}, u32[]{:S(2)}, u32[]{:S(2)}) async-start(bf16[16,80,256]{2,1,0:T(8,128)(2,1)} %route.3), calls=%async_computation.4 | async-start | bytes 1310720 | tf_op jit(solution)/shard_map/all_to_all | solution.py:552
  (4 other events, 14.3 us)
